TPU v7x, 128 devices: a whole 4x4x4 slice. The times are simulated.
128 devices in a mesh: ctx: 8 (over y_hi, x), fsdp: 16 (over z, y_lo, core).
Axes of the slice: x: 4, y: 4 (y_hi: 2, y_lo: 2; y = y_hi * 2 + y_lo), z: 4, core: 2. Of those that a mesh axis runs over, the one named last changes fastest.
Arguments:
- tokens: bfloat16 [16, 2, 512, 1536], P('fsdp', None, 'ctx'), may hold values from -6 to 6
- cotangent: bfloat16 [16, 2, 512, 1536], P('fsdp', None, 'ctx'), may hold values from -6 to 6
- attn_gain: bfloat16 [1536], P(('ctx', 'fsdp')), may hold values from 0.099609375 to 1.8984375
- q_weight: bfloat16 [1536, 1536], P(('ctx', 'fsdp')), may hold values from -0.15625 to 0.15625
- q_bias: bfloat16 [1536], P(('ctx', 'fsdp')), may hold values from -3 to 3
- k_weight: bfloat16 [1536, 256], P(('ctx', 'fsdp')), may hold values from -0.15625 to 0.15625
- k_bias: bfloat16 [256], P(('ctx', 'fsdp')), may hold values from -3 to 3
- v_weight: bfloat16 [1536, 256], P(('ctx', 'fsdp')), may hold values from -0.15625 to 0.15625
- v_bias: bfloat16 [256], P(('ctx', 'fsdp')), may hold values from -1.1953125 to 1.1953125
- o_weight: bfloat16 [1536, 1536], P(('ctx', 'fsdp')), may hold values from -0.75 to 0.75
- mlp_gain: bfloat16 [1536], P(('ctx', 'fsdp')), may hold values from 0.099609375 to 1.8984375
- gate_weight: bfloat16 [1536, 8960], P(('ctx', 'fsdp')), may hold values from -0.15625 to 0.15625
- up_weight: bfloat16 [1536, 8960], P(('ctx', 'fsdp')), may hold values from -0.15625 to 0.15625
- down_weight: bfloat16 [1536, 8960], P(('ctx', 'fsdp')), may hold values from -0.0625 to 0.0625
Outputs:
- layer_out: bfloat16 [16, 2, 512, 1536], P('fsdp', None, 'ctx')
- input_grad: float32 [16, 2, 512, 1536], P('fsdp', None, 'ctx')
- attn_gain_grad: float32 [1536], P(('ctx', 'fsdp'))
- q_weight_grad: float32 [1536, 1536], P(('ctx', 'fsdp'))
- q_bias_grad: float32 [1536], P(('ctx', 'fsdp'))
- k_weight_grad: float32 [1536, 256], P(('ctx', 'fsdp'))
- k_bias_grad: float32 [256], replicated
- v_weight_grad: float32 [1536, 256], P(('ctx', 'fsdp'))
- v_bias_grad: float32 [256], P(('ctx', 'fsdp'))
- o_weight_grad: float32 [1536, 1536], P(('ctx', 'fsdp'))
- mlp_gain_grad: float32 [1536], P(('ctx', 'fsdp'))
- gate_weight_grad: float32 [1536, 8960], P(('ctx', 'fsdp'))
- up_weight_grad: float32 [1536, 8960], P(('ctx', 'fsdp'))
- down_weight_grad: float32 [1536, 8960], P(('ctx', 'fsdp'))
All inputs are finite; a program needn't handle non-finite values.
Results may differ from a plain program's by a relative error of at most 0.029.
Values may be sent and summed in bfloat16 or wider, within the bound.
No kernel may reach another device: no remote copies, remote signals or barrier semaphores. Data moves between devices by JAX's collectives and lax.ppermute only.
A program may use at most 320 MiB of HBM per device.

v0:
```python
import math

import jax
import jax.numpy as jnp
from jax import lax
from jax.sharding import PartitionSpec as P

H = 12
KVH = 2
HD = 128


epsilon = 1e-06
rope_base = 1000000.0


def rope_tables(positions):
    half_dim = HD // 2
    frequency = jnp.exp(jnp.arange(half_dim, dtype=jnp.float32) * (-2.0 * math.log(rope_base) / HD))
    angles = positions.astype(jnp.float32)[:, None] * frequency[None, :]
    cosine_tab = jnp.cos(angles)
    sine_tab = jnp.sin(angles)
    return (
        jnp.concatenate([cosine_tab, cosine_tab], -1),
        jnp.concatenate([sine_tab, sine_tab], -1),
    )


def rotate(values, cosine_tab, sine_tab):
    half_dim = values.shape[-1] // 2
    turned = jnp.concatenate([-values[..., half_dim:], values[..., :half_dim]], -1)
    return values * cosine_tab + turned * sine_tab


def unrotate(grads_in, cosine_tab, sine_tab):
    half_dim = grads_in.shape[-1] // 2
    scaled = grads_in * sine_tab
    return grads_in * cosine_tab + jnp.concatenate(
        [scaled[..., half_dim:], -scaled[..., :half_dim]], -1
    )


def product(left_arr, right_arr):
    return jnp.dot(left_arr, right_arr, preferred_element_type=jnp.float32)


def against(left_arr, right_arr):
    return lax.dot_general(
        left_arr, right_arr, (((1,), (1,)), ((), ())), preferred_element_type=jnp.float32
    )


def over_rows(left_arr, right_arr):
    return lax.dot_general(
        left_arr, right_arr, (((0,), (0,)), ((), ())), preferred_element_type=jnp.float32
    )


def masked_scores(query_heads, key_heads, visible, score_scale):
    scores = (
        jnp.einsum("slkrd,smkd->skrlm", query_heads, key_heads, preferred_element_type=jnp.float32)
        * score_scale
    )
    return jnp.where(visible, scores, -jnp.inf)


def per_device(
    tokens,
    cotangent,
    attn_gain,
    q_weight,
    q_bias,
    k_weight,
    k_bias,
    v_weight,
    v_bias,
    o_weight,
    mlp_gain,
    gate_weight,
    up_weight,
    down_weight,
):
    seqs_here, _, block_len, width = tokens.shape
    n_ctx = lax.axis_size("ctx")
    n_fsdp = lax.axis_size("fsdp")
    ctx_rank = lax.axis_index("ctx")
    groups = H // KVH
    key_count = 2 * n_ctx * block_len
    local_len = 2 * block_len
    row_count = seqs_here * local_len
    score_scale = 1.0 / math.sqrt(HD)
    ff_width = gate_weight.shape[1]
    slice_width = width // n_ctx
    slice_start = ctx_rank * slice_width
    shard_rows = gate_weight.shape[0]
    gain_one, weight_q, bias_q, weight_k, bias_k, weight_v, bias_v, weight_o, gain_two = (
        lax.all_gather(attn_gain, ("ctx", "fsdp"), axis=0, tiled=True),
        lax.all_gather(q_weight, ("ctx", "fsdp"), axis=0, tiled=True),
        lax.all_gather(q_bias, ("ctx", "fsdp"), axis=0, tiled=True),
        lax.all_gather(k_weight, ("ctx", "fsdp"), axis=0, tiled=True),
        lax.all_gather(k_bias, ("ctx", "fsdp"), axis=0, tiled=True),
        lax.all_gather(v_weight, ("ctx", "fsdp"), axis=0, tiled=True),
        lax.all_gather(v_bias, ("ctx", "fsdp"), axis=0, tiled=True),
        lax.all_gather(o_weight, ("ctx", "fsdp"), axis=0, tiled=True),
        lax.all_gather(mlp_gain, ("ctx", "fsdp"), axis=0, tiled=True),
    )
    weight_gate, weight_up, weight_down = (
        lax.all_gather(gate_weight, ("ctx", "fsdp"), axis=0, tiled=True),
        lax.all_gather(up_weight, ("ctx", "fsdp"), axis=0, tiled=True),
        lax.all_gather(down_weight, ("ctx", "fsdp"), axis=0, tiled=True),
    )
    offsets = jnp.arange(block_len, dtype=jnp.int32)
    query_pos = jnp.concatenate(
        [ctx_rank * block_len + offsets, (2 * n_ctx - 1 - ctx_rank) * block_len + offsets]
    )
    slots = jnp.arange(n_ctx * block_len, dtype=jnp.int32)
    key_pos = jnp.concatenate(
        [slots, (2 * n_ctx - 1 - slots // block_len) * block_len + slots % block_len]
    )
    visible = query_pos[:, None] >= key_pos[None, :]
    cosine_tab, sine_tab = rope_tables(query_pos)
    cosine_b = cosine_tab[None, :, None, :]
    sine_b = sine_tab[None, :, None, :]
    inputs = tokens.astype(jnp.float32).reshape(row_count, width)
    grad_out = cotangent.astype(jnp.float32).reshape(row_count, width)
    grad_low = cotangent.reshape(row_count, width)
    scale_one = lax.rsqrt(jnp.mean(inputs * inputs, axis=-1, keepdims=True) + epsilon)
    unit_one = inputs * scale_one
    normed_one = (unit_one * gain_one.astype(jnp.float32)).astype(jnp.bfloat16)
    query_lin = product(normed_one, weight_q) + bias_q.astype(jnp.float32)
    key_lin = product(normed_one, weight_k) + bias_k.astype(jnp.float32)
    value_low = (product(normed_one, weight_v) + bias_v.astype(jnp.float32)).astype(jnp.bfloat16)
    query_rot = rotate(query_lin.reshape(seqs_here, local_len, H, HD), cosine_b, sine_b).astype(
        jnp.bfloat16
    )
    key_rot = rotate(key_lin.reshape(seqs_here, local_len, KVH, HD), cosine_b, sine_b).astype(
        jnp.bfloat16
    )
    key_send = key_rot.reshape(seqs_here, 2, block_len, KVH * HD)
    value_send = value_low.reshape(seqs_here, 2, block_len, KVH * HD)
    key_all, value_all = (
        lax.all_gather(key_send, "ctx", axis=2, tiled=True),
        lax.all_gather(value_send, "ctx", axis=2, tiled=True),
    )
    key_heads = key_all.reshape(seqs_here, key_count, KVH, HD)
    value_heads = value_all.reshape(seqs_here, key_count, KVH, HD)
    query_heads = query_rot.reshape(seqs_here, local_len, KVH, groups, HD)
    masked = masked_scores(query_heads, key_heads, visible, score_scale)
    row_max = jnp.max(masked, axis=-1, keepdims=True)
    exp_terms = jnp.exp(masked - row_max)
    row_sum = jnp.sum(exp_terms, axis=-1, keepdims=True)
    probs_low = (exp_terms / row_sum).astype(jnp.bfloat16)
    context = jnp.einsum(
        "skrlm,smkd->slkrd", probs_low, value_heads, preferred_element_type=jnp.float32
    )
    context_low = context.reshape(row_count, H * HD).astype(jnp.bfloat16)
    hidden_one = inputs + against(context_low, weight_o)
    scale_two = lax.rsqrt(jnp.mean(hidden_one * hidden_one, axis=-1, keepdims=True) + epsilon)
    unit_two = hidden_one * scale_two
    normed_two = (unit_two * gain_two.astype(jnp.float32)).astype(jnp.bfloat16)
    gate_val = product(normed_two, weight_gate)
    up_val = product(normed_two, weight_up)
    gate_sig = jax.nn.sigmoid(gate_val)
    swish = gate_val * gate_sig
    mixed_low = (swish * up_val).astype(jnp.bfloat16)
    down_terms = against(mixed_low, weight_down)
    layer_out = (hidden_one + down_terms).astype(jnp.bfloat16).reshape(tokens.shape)
    gain_one_f = gain_one.astype(jnp.float32)
    gain_two_f = gain_two.astype(jnp.float32)
    grad_mixed = product(grad_low, weight_down)
    grad_up = (grad_mixed * swish).astype(jnp.bfloat16)
    grad_gate = (grad_mixed * up_val * gate_sig * (1.0 + gate_val * (1.0 - gate_sig))).astype(
        jnp.bfloat16
    )
    grad_norm_two = against(grad_gate, weight_gate) + against(grad_up, weight_up)
    normed_rows, grad_rows, gate_rows, up_rows, mixed_rows = (
        lax.all_gather(normed_two, "ctx", axis=0, tiled=True),
        lax.all_gather(grad_low, "ctx", axis=0, tiled=True),
        lax.all_gather(grad_gate, "ctx", axis=0, tiled=True),
        lax.all_gather(grad_up, "ctx", axis=0, tiled=True),
        lax.all_gather(mixed_low, "ctx", axis=0, tiled=True),
    )
    left_cols = lax.dynamic_slice_in_dim(
        normed_rows, slice_start, shard_rows * lax.axis_size("fsdp"), 1
    )
    down_cols = lax.dynamic_slice_in_dim(
        grad_rows, slice_start, shard_rows * lax.axis_size("fsdp"), 1
    )
    mlp_grads = lax.psum_scatter(
        jnp.concatenate(
            [
                over_rows(left_cols, gate_rows),
                over_rows(left_cols, up_rows),
                over_rows(down_cols, mixed_rows),
            ],
            axis=1,
        ).astype(jnp.bfloat16),
        "fsdp",
        scatter_dimension=0,
        tiled=True,
    ).astype(jnp.float32)
    gate_weight_grad = mlp_grads[:, :ff_width]
    up_weight_grad = mlp_grads[:, ff_width : 2 * ff_width]
    down_weight_grad = mlp_grads[:, 2 * ff_width :]
    gain_two_term = jnp.sum(grad_norm_two * unit_two, axis=0)
    grad_unit_two = grad_norm_two * gain_two_f
    grad_hidden = grad_out + scale_two * (
        grad_unit_two - unit_two * jnp.mean(grad_unit_two * unit_two, axis=-1, keepdims=True)
    )
    grad_branch = grad_hidden.astype(jnp.bfloat16)
    grad_context = product(grad_branch, weight_o).astype(jnp.bfloat16)
    grad_ctx_heads = grad_context.reshape(seqs_here, local_len, KVH, groups, HD)
    again_masked = masked_scores(query_heads, key_heads, visible, score_scale)
    probs = jnp.exp(again_masked - row_max) / row_sum
    probs_again = probs.astype(jnp.bfloat16)
    grad_probs = jnp.einsum(
        "slkrd,smkd->skrlm", grad_ctx_heads, value_heads, preferred_element_type=jnp.float32
    )
    row_delta = jnp.sum(probs * grad_probs, axis=-1, keepdims=True)
    grad_scores = (probs * (grad_probs - row_delta)).astype(jnp.bfloat16)
    grad_query = (
        jnp.einsum("skrlm,smkd->slkrd", grad_scores, key_heads, preferred_element_type=jnp.float32)
        * score_scale
    )
    grad_key_all = (
        jnp.einsum(
            "skrlm,slkrd->smkd", grad_scores, query_heads, preferred_element_type=jnp.float32
        )
        * score_scale
    )
    grad_value_all = jnp.einsum(
        "skrlm,slkrd->smkd", probs_again, grad_ctx_heads, preferred_element_type=jnp.float32
    )
    grad_key, grad_value = (
        lax.psum_scatter(
            grad_key_all.reshape(seqs_here, 2, n_ctx * block_len, KVH * HD).astype(jnp.bfloat16),
            "ctx",
            scatter_dimension=2,
            tiled=True,
        ).astype(jnp.float32),
        lax.psum_scatter(
            grad_value_all.reshape(seqs_here, 2, n_ctx * block_len, KVH * HD).astype(jnp.bfloat16),
            "ctx",
            scatter_dimension=2,
            tiled=True,
        ).astype(jnp.float32),
    )
    grad_q_lin = (
        unrotate(grad_query.reshape(seqs_here, local_len, H, HD), cosine_b, sine_b)
        .reshape(row_count, H * HD)
        .astype(jnp.bfloat16)
    )
    grad_k_lin = (
        unrotate(grad_key.reshape(seqs_here, local_len, KVH, HD), cosine_b, sine_b)
        .reshape(row_count, KVH * HD)
        .astype(jnp.bfloat16)
    )
    grad_v_lin = grad_value.reshape(row_count, KVH * HD).astype(jnp.bfloat16)
    grad_norm_one = (
        against(grad_q_lin, weight_q)
        + against(grad_k_lin, weight_k)
        + against(grad_v_lin, weight_v)
    )
    gain_one_term = jnp.sum(grad_norm_one * unit_one, axis=0)
    grad_unit_one = grad_norm_one * gain_one_f
    input_grad = grad_hidden + scale_one * (
        grad_unit_one - unit_one * jnp.mean(grad_unit_one * unit_one, axis=-1, keepdims=True)
    )
    input_grad = input_grad.reshape(tokens.shape)
    normed_gathered, grad_q_rows, grad_k_rows, grad_v_rows, branch_rows, context_rows = (
        lax.all_gather(normed_one, "ctx", axis=0, tiled=True),
        lax.all_gather(grad_q_lin, "ctx", axis=0, tiled=True),
        lax.all_gather(grad_k_lin, "ctx", axis=0, tiled=True),
        lax.all_gather(grad_v_lin, "ctx", axis=0, tiled=True),
        lax.all_gather(grad_branch, "ctx", axis=0, tiled=True),
        lax.all_gather(context_low, "ctx", axis=0, tiled=True),
    )
    left_cols = lax.dynamic_slice_in_dim(
        normed_gathered, slice_start, shard_rows * lax.axis_size("fsdp"), 1
    )
    branch_cols = lax.dynamic_slice_in_dim(
        branch_rows, slice_start, shard_rows * lax.axis_size("fsdp"), 1
    )
    attn_grads = lax.psum_scatter(
        jnp.concatenate(
            [
                over_rows(left_cols, grad_q_rows),
                over_rows(left_cols, grad_k_rows),
                over_rows(left_cols, grad_v_rows),
                over_rows(branch_cols, context_rows),
            ],
            axis=1,
        ).astype(jnp.bfloat16),
        "fsdp",
        scatter_dimension=0,
        tiled=True,
    ).astype(jnp.float32)
    q_width = H * HD
    kv_width = KVH * HD
    q_weight_grad = attn_grads[:, :q_width]
    k_weight_grad = attn_grads[:, q_width : q_width + kv_width]
    v_weight_grad = attn_grads[:, q_width + kv_width : q_width + 2 * kv_width]
    o_weight_grad = attn_grads[:, q_width + 2 * kv_width :]
    q_bias_term = jnp.sum(grad_q_lin.astype(jnp.float32), axis=0)
    k_bias_term = jnp.sum(grad_k_lin.astype(jnp.float32), axis=0)
    v_bias_term = jnp.sum(grad_v_lin.astype(jnp.float32), axis=0)
    gain_one_sum, q_bias_sum, k_bias_grad, v_bias_sum, gain_two_sum = lax.psum(
        (gain_one_term, q_bias_term, k_bias_term, v_bias_term, gain_two_term), ("ctx", "fsdp")
    )
    flat_rank = ctx_rank * n_fsdp + lax.axis_index("fsdp")
    shard_count = n_ctx * n_fsdp

    def own_share(whole):
        share_len = whole.shape[0] // shard_count
        return lax.dynamic_slice_in_dim(whole, flat_rank * share_len, share_len, 0)

    attn_gain_grad = own_share(gain_one_sum)
    q_bias_grad = own_share(q_bias_sum)
    v_bias_grad = own_share(v_bias_sum)
    mlp_gain_grad = own_share(gain_two_sum)
    return (
        layer_out,
        input_grad,
        attn_gain_grad,
        q_weight_grad,
        q_bias_grad,
        k_weight_grad,
        k_bias_grad,
        v_weight_grad,
        v_bias_grad,
        o_weight_grad,
        mlp_gain_grad,
        gate_weight_grad,
        up_weight_grad,
        down_weight_grad,
    )


def solution(mesh):
    placed = (
        P("fsdp", None, "ctx", None),
        P("fsdp", None, "ctx", None),
        P(("ctx", "fsdp")),
        P(("ctx", "fsdp"), None),
        P(("ctx", "fsdp")),
        P(("ctx", "fsdp"), None),
        P(("ctx", "fsdp")),
        P(("ctx", "fsdp"), None),
        P(("ctx", "fsdp")),
        P(("ctx", "fsdp"), None),
        P(("ctx", "fsdp")),
        P(("ctx", "fsdp"), None),
        P(("ctx", "fsdp"), None),
        P(("ctx", "fsdp"), None),
    )
    return jax.shard_map(
        per_device,
        mesh=mesh,
        in_specs=placed,
        out_specs=(
            P("fsdp", None, "ctx", None),
            P("fsdp", None, "ctx", None),
            P(("ctx", "fsdp")),
            P(("ctx", "fsdp"), None),
            P(("ctx", "fsdp")),
            P(("ctx", "fsdp"), None),
            P(),
            P(("ctx", "fsdp"), None),
            P(("ctx", "fsdp")),
            P(("ctx", "fsdp"), None),
            P(("ctx", "fsdp")),
            P(("ctx", "fsdp"), None),
            P(("ctx", "fsdp"), None),
            P(("ctx", "fsdp"), None),
        ),
        check_vma=False,
    )
```

profile of v0, /device:TPU:1, one launch (start us, length us, event | category | flops | bytes accessed | tf_op | source)
XLA Modules:
  0.0 2766.2 jit_solution(3643294964261837994)
XLA Ops:
  16.1 69.1 %all-reduce.10 = (bf16[1536]{0:T(1024)(128)(2,1)S(1)}, bf16[256]{0:T(256)(128)(2,1)S(1)}, bf16[256]{0:T(256)(128)(2,1)S(1)}, bf16[1536]{0:T(1024)(128)(2,1)S(1)}, bf16[1536]{0:T(1024)(128)(2,1)S(1)}) all-reduce(bf16[1536]{0:T(1024)(128)(2,1)S(1)} %dynamic-update-slice, ...), channel_id=1, replica_groups=mesh['ctx'=8,'fsdp'=16] {'ctx','fsdp'}, use_global_device_ids=true, to_apply=%add | all-reduce | flops 5120 | bytes 20480
  86.8 176.5 %all-gather.1 = bf16[128,12,256]{2,1,0:T(8,128)(2,1)S(1)} all-gather(bf16[1,12,256]{2,1,0:T(8,128)(2,1)} %bitcast.245), channel_id=1, replica_groups=mesh['ctx'=8,'fsdp'=16] {'ctx','fsdp'}, dimensions={0}, use_global_device_ids=true | all-gather | bytes 792576 | tf_op jit(solution)/shard_map/all_gather | solution.py:100
  264.6 28.7 %all_gather.81 = bf16[1,2,512,256]{3,2,1,0:T(8,128)(2,1)S(1)} all-gather(bf16[1,2,64,256]{3,2,1,0:T(8,128)(2,1)S(1)} %add_convert_fusion.1), channel_id=1, replica_groups=mesh['ctx'=8,'fsdp'=16] {'ctx'}, dimensions={2}, use_global_device_ids=true | all-gather | bytes 589824 | tf_op jit(solution)/shard_map/all_gather | solution.py:142
  295.6 189.5 %all-gather = bf16[128,12,256]{2,1,0:T(8,128)(2,1)} all-gather(bf16[1,12,256]{2,1,0:T(8,128)(2,1)S(1)} %bitcast.246), channel_id=1, replica_groups=mesh['ctx'=8,'fsdp'=16] {'ctx','fsdp'}, dimensions={0}, use_global_device_ids=true | all-gather | bytes 792576 | tf_op jit(solution)/shard_map/all_gather | solution.py:102
  486.7 31.3 %all_gather.78 = bf16[1,2,512,256]{3,2,1,0:T(8,128)(2,1)} all-gather(bf16[1,2,64,256]{3,2,1,0:T(8,128)(2,1)S(1)} %bitcast.242), channel_id=1, replica_groups=mesh['ctx'=8,'fsdp'=16] {'ctx'}, dimensions={2}, use_global_device_ids=true | all-gather | bytes 589824 | tf_op jit(solution)/shard_map/all_gather | solution.py:143
  520.5 8.3 reshape.442
  528.8 4.1 convolution_add_fusion.3
  534.4 8.2 reshape.444
  547.2 4.4 multiply_reduce_fusion.4
  551.7 108.2 %all-gather.44.cloned.1.call-done = bf16[128,12,8960]{2,1,0:T(8,128)(2,1)} async-done(((bf16[1,12,8960]{2,1,0:T(8,128)(2,1)}), bf16[128,12,8960]{2,1,0:T(8,128)(2,1)}) %all-gather.44.cloned.1.call-update) | async-done | bytes 27525136 | tf_op jit(solution)/shard_map/all_gather | solution.py:108
  659.9 35.1 %reshape.446 = bf16[1536,8960]{1,0:T(8,128)(2,1)} reshape(bf16[128,12,8960]{2,1,0:T(8,128)(2,1)} %all-gather.44.cloned.1.call-done) | data formatting | bytes 55050240
  695.0 204.4 %all-gather.46.cloned.1.call-done = bf16[128,12,8960]{2,1,0:T(8,128)(2,1)} async-done(((bf16[1,12,8960]{2,1,0:T(8,128)(2,1)}), bf16[128,12,8960]{2,1,0:T(8,128)(2,1)}) %all-gather.46.cloned.1.call-update) | async-done | bytes 27525136 | tf_op jit(solution)/shard_map/all_gather | solution.py:109
  899.4 35.5 %reshape.448 = bf16[1536,8960]{1,0:T(8,128)(2,1)} reshape(bf16[128,12,8960]{2,1,0:T(8,128)(2,1)} %all-gather.46.cloned.1.call-done) | data formatting | bytes 55050240
  935.0 15.2 fusion.75
  950.2 15.2 fusion.74
  965.4 173.6 %all-gather.48.cloned.1.call-done = bf16[128,12,8960]{2,1,0:T(8,128)(2,1)} async-done(((bf16[1,12,8960]{2,1,0:T(8,128)(2,1)}), bf16[128,12,8960]{2,1,0:T(8,128)(2,1)}) %all-gather.48.cloned.1.call-update) | async-done | bytes 27525136 | tf_op jit(solution)/shard_map/all_gather | solution.py:110
  1139.1 34.8 %reshape.450 = bf16[1536,8960]{1,0:T(8,128)(2,1)} reshape(bf16[128,12,8960]{2,1,0:T(8,128)(2,1)} %all-gather.48.cloned.1.call-done) | data formatting | bytes 55050240
  1173.9 16.5 multiply_convert_fusion
  1190.4 15.6 fusion.76
  1206.0 15.5 multiply_reduce_fusion
  1227.0 4.4 fusion.2
  1238.0 5.7 fusion.27
  1261.3 4.9 fusion.77
  1266.2 14.7 fusion.15
  1281.0 24.7 reduce-scatter.7.cloned.1.call-done
  1312.3 67.9 %reduce-scatter.9.cloned.1.call-done = bf16[1,2,64,256]{3,2,1,0:T(8,128)(2,1)} async-done(((bf16[1,2,512,256]{3,2,1,0:T(8,128)(2,1)}), bf16[1,2,64,256]{3,2,1,0:T(8,128)(2,1)}) %reduce-scatter.9.cloned.1.call-update) | async-done | bytes 65552 | tf_op jit(solution)/shard_map/reduce_scatter | solution.py:241
  1382.7 31.8 %all_gather.92 = bf16[1024,256]{1,0:T(8,128)(2,1)} all-gather(bf16[128,256]{1,0:T(8,128)(2,1)} %bitcast.235), channel_id=1, replica_groups=mesh['ctx'=8,'fsdp'=16] {'ctx'}, dimensions={0}, use_global_device_ids=true | all-gather | bytes 589824 | tf_op jit(solution)/shard_map/all_gather | solution.py:274
  1414.5 30.6 %all_gather.91 = bf16[1024,256]{1,0:T(8,128)(2,1)S(1)} all-gather(bf16[128,256]{1,0:T(8,128)(2,1)S(1)} %fusion.46), channel_id=1, replica_groups=mesh['ctx'=8,'fsdp'=16] {'ctx'}, dimensions={0}, use_global_device_ids=true | all-gather | bytes 589824 | tf_op jit(solution)/shard_map/all_gather | solution.py:273
  1445.1 5.0 all-gather.22.cloned.1.call-done
  1456.1 62.1 %all-gather.24.cloned.1.call-done = bf16[1024,1536]{0,1:T(8,128)(2,1)} async-done(((bf16[128,1536]{0,1:T(8,128)(2,1)}), bf16[1024,1536]{0,1:T(8,128)(2,1)}) %all-gather.24.cloned.1.call-update) | async-done | bytes 3145744 | tf_op jit(solution)/shard_map/all_gather | solution.py:272
  1521.8 64.9 %all-gather.28.cloned.1.call-done = bf16[1024,1536]{0,1:T(8,128)(2,1)} async-done(((bf16[128,1536]{0,1:T(8,128)(2,1)}), bf16[1024,1536]{0,1:T(8,128)(2,1)}) %all-gather.28.cloned.1.call-update) | async-done | bytes 3145744 | tf_op jit(solution)/shard_map/all_gather | solution.py:276
  1586.7 64.7 %all-gather.26.cloned.1.call-done = bf16[1024,1536]{1,0:T(8,128)(2,1)} async-done(((bf16[128,1536]{1,0:T(8,128)(2,1)}), bf16[1024,1536]{1,0:T(8,128)(2,1)}) %all-gather.26.cloned.1.call-update) | async-done | bytes 3145744 | tf_op jit(solution)/shard_map/all_gather | solution.py:275
  1656.2 58.9 %all-gather.30.cloned.1.call-done = bf16[1024,1536]{1,0:T(8,128)(2,1)} async-done(((bf16[128,1536]{1,0:T(8,128)(2,1)}), bf16[1024,1536]{1,0:T(8,128)(2,1)}) %all-gather.30.cloned.1.call-update) | async-done | bytes 3145744 | tf_op jit(solution)/shard_map/all_gather | solution.py:177
  1715.1 201.2 %all-gather.34.cloned.1.call-done = bf16[1024,8960]{1,0:T(8,128)(2,1)} async-done(((bf16[128,8960]{1,0:T(8,128)(2,1)}), bf16[1024,8960]{1,0:T(8,128)(2,1)}) %all-gather.34.cloned.1.call-update) | async-done | bytes 18350096 | tf_op jit(solution)/shard_map/all_gather | solution.py:180
  1916.4 10.3 convolution_convert_fusion.1
  1926.7 190.2 %all-gather.32.cloned.1.call-done = bf16[1024,8960]{1,0:T(8,128)(2,1)} async-done(((bf16[128,8960]{1,0:T(8,128)(2,1)}), bf16[1024,8960]{1,0:T(8,128)(2,1)}) %all-gather.32.cloned.1.call-update) | async-done | bytes 18350096 | tf_op jit(solution)/shard_map/all_gather | solution.py:179
  2116.9 12.0 convolution_convert_fusion.2
  2128.9 51.1 %all-gather.36.cloned.1.call-done = bf16[1024,1536]{1,0:T(8,128)(2,1)} async-done(((bf16[128,1536]{1,0:T(8,128)(2,1)}), bf16[1024,1536]{1,0:T(8,128)(2,1)}) %all-gather.36.cloned.1.call-update) | async-done | bytes 3145744 | tf_op jit(solution)/shard_map/all_gather | solution.py:178
  2180.0 201.1 %all-gather.38.cloned.1.call-done = bf16[1024,8960]{1,0:T(8,128)(2,1)} async-done(((bf16[128,8960]{1,0:T(8,128)(2,1)}), bf16[1024,8960]{1,0:T(8,128)(2,1)}) %all-gather.38.cloned.1.call-update) | async-done | bytes 18350096 | tf_op jit(solution)/shard_map/all_gather | solution.py:181
  2381.1 10.7 convolution_convert_fusion
  2391.8 7.5 pad_maximum_fusion
  2399.4 161.7 %fusion.67 = (bf16[16,3584]{1,0:T(8,128)(2,1)S(1)}, bf16[16,26880]{1,0:T(8,128)(2,1)S(1)}) fusion(bf16[192,3584]{1,0:T(8,128)(2,1)} %pad_maximum_fusion.1, bf16[192,26880]{1,0:T(8,128)(2,1)} %pad_maximum_fusion), kind=kCustom, calls=%all-reduce-scatter.2 | all-reduce-scatter fusion | flops 7798785 | bytes 12673536
  2561.1 5.5 collective-permute-start.2
  2574.5 64.2 %all-reduce.9 = (f32[1536]{0:T(1024)S(1)}, f32[1536]{0:T(1024)S(1)}, f32[256]{0:T(256)}, f32[256]{0:T(256)S(1)}, f32[1536]{0:T(1024)S(1)}) all-reduce(f32[1536]{0:T(1024)S(1)} %get-tuple-element.16, f32[1536]{0:T(1024)S(1)} %copy-done.50, f32[256]{0:T(256)S(1)} %copy-done.56, ...), channel_id=1, replica_groups=mesh['ctx'=8,'fsdp'=16] {'ctx','fsdp'}, use_global_device_ids=true, to_apply=%region_10.11 | all-reduce | flops 5120 | bytes 40960 | tf_op jit(solution)/shard_map/psum | solution.py:307
  2648.8 4.4 collective-permute-start.7
  2653.2 11.4 concatenate.89
  2666.8 41.5 %collective-permute-done.7 = bf16[12,26880]{1,0:T(8,128)(2,1)} collective-permute-done((bf16[12,26880]{1,0:T(8,128)(2,1)S(1)}, bf16[12,26880]{1,0:T(8,128)(2,1)}, u32[]{:S(2)}, u32[]{:S(2)}) %collective-permute-start.7) | collective-permute-done | bytes 645152
  2708.3 48.4 %concatenate.90 = bf16[76,26880]{1,0:T(8,128)(2,1)} concatenate(bf16[12,26880]{1,0:T(8,128)(2,1)} %collective-permute-done.7, bf16[16,26880]{1,0:T(8,128)(2,1)S(1)} %collective-permute-done.6, bf16[16,26880]{1,0:T(8,128)(2,1)S(1)} %collective-permute-done.5, bf16[16,26880]{1,0:T(8,128)(2,1)} %collective-permute-done.4, bf16[16,26880]{1,0:T(8,128)(2,1)S(1)} %get-tuple-element.31), dimensions={0} | concatenate | bytes 8171520
  (274 shorter events, 98.8 us)
Async XLA Ops:
  7.2 256.3 %copy-start.8 = (bf16[1,2,64,1536]{3,2,1,0:T(8,128)(2,1)S(1)}, bf16[1,2,64,1536]{3,2,1,0:T(8,128)(2,1)}, u32[]{:S(2)}) copy-start(bf16[1,2,64,1536]{3,2,1,0:T(8,128)(2,1)} %param.14) | copy-start | bytes 1179652
  7.2 513.3 %all-gather.40.cloned.1.call-start = ((), (), s32[]{:S(2)}) async-start(), calls=%async_computation.13 | async-start | bytes 6340608 | tf_op jit(solution)/shard_map/all_gather | solution.py:98
  7.9 526.4 %all-gather.42.cloned.1.call-start = ((), (), s32[]{:S(2)}) async-start(), calls=%async_computation.14 | async-start | bytes 6340608 | tf_op jit(solution)/shard_map/all_gather | solution.py:104
  8.7 651.2 %all-gather.44.cloned.1.call-start = ((), (), s32[]{:S(2)}) async-start(), calls=%async_computation.15 | async-start | bytes 36986880 | tf_op jit(solution)/shard_map/all_gather | solution.py:108
  9.4 890.0 %all-gather.46.cloned.1.call-start = ((), (), s32[]{:S(2)}) async-start(), calls=%async_computation.16 | async-start | bytes 36986880 | tf_op jit(solution)/shard_map/all_gather | solution.py:109
  10.0 1129.1 %all-gather.48.cloned.1.call-start = ((), (), s32[]{:S(2)}) async-start(), calls=%async_computation.17 | async-start | bytes 36986880 | tf_op jit(solution)/shard_map/all_gather | solution.py:110
  10.6 1295.1 %reduce-scatter.7.cloned.1.call-start = ((), (), s32[]{:S(2)}) async-start(), calls=%async_computation.2 | async-start | bytes 589824 | tf_op jit(solution)/shard_map/reduce_scatter | solution.py:235
  11.9 252.4 %copy-start.54 = (f32[128]{0:T(128)}, f32[128]{0:T(128)S(1)}, u32[]{:S(2)}) copy-start(f32[128]{0:T(128)S(1)} %rsqrt.20) | copy-start | bytes 1540
  85.3 179.0 %copy-start.45 = (f32[1536]{0:T(1024)}, f32[1536]{0:T(1024)S(1)}, u32[]{:S(2)}) copy-start(f32[1536]{0:T(1024)S(1)} %convert_element_type.188) | copy-start | bytes 18436
  85.6 457.1 %copy-start.38 = (f32[128,128]{0,1:T(8,128)}, f32[128,128]{0,1:T(8,128)S(1)}, u32[]{:S(2)}) copy-start(f32[128,128]{0,1:T(8,128)S(1)} %pad_maximum_fusion.6) | copy-start | bytes 196612
  85.7 177.6 %copy-start.40 = (f32[128,128]{1,0:T(8,128)}, f32[128,128]{1,0:T(8,128)S(1)}, u32[]{:S(2)}) copy-start(f32[128,128]{1,0:T(8,128)S(1)} %copy.65) | copy-start | bytes 196612
  86.4 456.3 %copy-start.36 = (f32[128,128]{0,1:T(8,128)}, f32[128,128]{0,1:T(8,128)S(1)}, u32[]{:S(2)}) copy-start(f32[128,128]{0,1:T(8,128)S(1)} %get-tuple-element.53) | copy-start | bytes 196612
  86.5 176.8 %copy-start.32 = (f32[128,2,128]{2,1,0:T(2,128)}, f32[128,2,128]{2,1,0:T(2,128)S(1)}, u32[]{:S(2)}) copy-start(f32[128,2,128]{2,1,0:T(2,128)S(1)} %mul.340) | copy-start | bytes 393220
  86.7 208.9 %copy-start.34 = (f32[1,2,64,256]{3,2,1,0:T(8,128)}, f32[1,2,64,256]{3,2,1,0:T(8,128)S(1)}, u32[]{:S(2)}) copy-start(f32[1,2,64,256]{3,2,1,0:T(8,128)S(1)} %mul.341) | copy-start | bytes 393220
  86.8 208.7 %copy-start.51 = (bf16[12,256]{1,0:T(8,128)(2,1)S(1)}, bf16[12,256]{1,0:T(8,128)(2,1)}, u32[]{:S(2)}) copy-start(bf16[12,256]{1,0:T(8,128)(2,1)} %param.21) | copy-start | bytes 18436
  263.5 222.9 %copy-start.11 = (bf16[1536,256]{1,0:T(8,128)(2,1)}, bf16[1536,256]{1,0:T(8,128)(2,1)S(1)}, u32[]{:S(2)}) copy-start(bf16[1536,256]{1,0:T(8,128)(2,1)S(1)} %reshape.440) | copy-start | bytes 2359300
  263.7 265.2 %copy-start.10 = (bf16[128,1536]{1,0:T(8,128)(2,1)}, bf16[128,1536]{1,0:T(8,128)(2,1)S(1)}, u32[]{:S(2)}) copy-start(bf16[128,1536]{1,0:T(8,128)(2,1)S(1)} %multiply_convert_fusion.4) | copy-start | bytes 1179652
  295.6 247.3 %copy-start.17 = (bf16[1024,2,128,1]{0,2,3,1:T(8,128)(2,1)}, bf16[1024,2,128,1]{0,2,3,1:T(8,128)(2,1)S(1)}, u32[]{:S(2)}) copy-start(bf16[1024,2,128,1]{0,2,3,1:T(8,128)(2,1)S(1)} %copy.87) | copy-start | bytes 1572868
  547.2 147.9 %copy-start.31 = (bf16[2,128,6,128]{3,1,2,0:T(8,128)(2,1)}, bf16[2,128,6,128]{3,1,2,0:T(8,128)(2,1)S(1)}, u32[]{:S(2)}) copy-start(bf16[2,128,6,128]{3,1,2,0:T(8,128)(2,1)S(1)} %fusion.24) | copy-start | bytes 1179652
  551.5 670.0 %copy-start.3 = (f32[128,1536]{1,0:T(8,128)}, f32[128,1536]{1,0:T(8,128)S(1)}, u32[]{:S(2)}) copy-start(f32[128,1536]{1,0:T(8,128)S(1)} %get-tuple-element.59) | copy-start | bytes 2359300
  551.6 654.5 %copy-start.52 = (f32[128]{0:T(128)}, f32[128]{0:T(128)S(1)}, u32[]{:S(2)}) copy-start(f32[128]{0:T(128)S(1)} %add_rsqrt_fusion.1) | copy-start | bytes 1540
  551.7 398.5 %copy-start.16 = (bf16[128,1536]{1,0:T(8,128)(2,1)}, bf16[128,1536]{1,0:T(8,128)(2,1)S(1)}, u32[]{:S(2)}) copy-start(bf16[128,1536]{1,0:T(8,128)(2,1)S(1)} %multiply_convert_fusion.3) | copy-start | bytes 1179652
  965.4 208.5 %copy-start.20 = (bf16[1,2,64,1536]{3,2,1,0:T(8,128)(2,1)S(1)}, bf16[1,2,64,1536]{3,2,1,0:T(8,128)(2,1)}, u32[]{:S(2)}) copy-start(bf16[1,2,64,1536]{3,2,1,0:T(8,128)(2,1)} %param.15) | copy-start | bytes 1179652
  1237.9 142.2 %reduce-scatter.9.cloned.1.call-start = ((), (), s32[]{:S(2)}) async-start(), calls=%async_computation.3 | async-start | bytes 589824 | tf_op jit(solution)/shard_map/reduce_scatter | solution.py:241
  1247.9 202.2 %all-gather.22.cloned.1.call-start = ((), (), s32[]{:S(2)}) async-start(), calls=%async_computation.4 | async-start | bytes 3538944 | tf_op jit(solution)/shard_map/all_gather | solution.py:271
  1248.7 269.5 %all-gather.24.cloned.1.call-start = ((), (), s32[]{:S(2)}) async-start(), calls=%async_computation.5 | async-start | bytes 3538944 | tf_op jit(solution)/shard_map/all_gather | solution.py:272
  1253.3 333.4 %all-gather.28.cloned.1.call-start = ((), (), s32[]{:S(2)}) async-start(), calls=%async_computation.7 | async-start | bytes 3538944 | tf_op jit(solution)/shard_map/all_gather | solution.py:276
  1253.9 397.5 %all-gather.26.cloned.1.call-start = ((), (), s32[]{:S(2)}) async-start(), calls=%async_computation.6 | async-start | bytes 3538944 | tf_op jit(solution)/shard_map/all_gather | solution.py:275
  1254.6 460.5 %all-gather.30.cloned.1.call-start = ((), (), s32[]{:S(2)}) async-start(), calls=%async_computation.8 | async-start | bytes 3538944 | tf_op jit(solution)/shard_map/all_gather | solution.py:177
  1255.2 661.1 %all-gather.34.cloned.1.call-start = ((), (), s32[]{:S(2)}) async-start(), calls=%async_computation.10 | async-start | bytes 20643840 | tf_op jit(solution)/shard_map/all_gather | solution.py:180
  1256.0 860.9 %all-gather.32.cloned.1.call-start = ((), (), s32[]{:S(2)}) async-start(), calls=%async_computation.9 | async-start | bytes 20643840 | tf_op jit(solution)/shard_map/all_gather | solution.py:179
  1256.5 923.5 %all-gather.36.cloned.1.call-start = ((), (), s32[]{:S(2)}) async-start(), calls=%async_computation.11 | async-start | bytes 3538944 | tf_op jit(solution)/shard_map/all_gather | solution.py:178
  1257.1 1124.0 %all-gather.38.cloned.1.call-start = ((), (), s32[]{:S(2)}) async-start(), calls=%async_computation.12 | async-start | bytes 20643840 | tf_op jit(solution)/shard_map/all_gather | solution.py:181
  1308.7 144.9 %copy-start.53 = (f32[128]{0:T(128)S(1)}, f32[128]{0:T(128)}, u32[]{:S(2)}) copy-start(f32[128]{0:T(128)} %copy-done.52) | copy-start | bytes 1540
  1308.7 144.9 %copy-start.55 = (f32[128]{0:T(128)S(1)}, f32[128]{0:T(128)}, u32[]{:S(2)}) copy-start(f32[128]{0:T(128)} %copy-done.54) | copy-start | bytes 1540
  1308.7 144.9 %copy-start.58 = (f32[128]{0:T(128)S(1)}, f32[128]{0:T(128)}, u32[]{:S(2)}) copy-start(f32[128]{0:T(128)} %copy-done.57) | copy-start | bytes 1540
  2399.3 175.1 %copy-start.42 = (bf16[1,2,64,256]{3,2,1,0:T(8,128)(2,1)S(1)}, bf16[1,2,64,256]{3,2,1,0:T(8,128)(2,1)}, u32[]{:S(2)}) copy-start(bf16[1,2,64,256]{3,2,1,0:T(8,128)(2,1)} %reduce-scatter.9.cloned.1.call-done) | copy-start | bytes 196612
  2399.3 175.1 %copy-start.49 = (f32[1536]{0:T(1024)S(1)}, f32[1536]{0:T(1024)}, u32[]{:S(2)}) copy-start(f32[1536]{0:T(1024)} %get-tuple-element.14) | copy-start | bytes 18436
  2399.3 175.1 %copy-start.50 = (f32[1536]{0:T(1024)S(1)}, f32[1536]{0:T(1024)}, u32[]{:S(2)}) copy-start(f32[1536]{0:T(1024)} %reduce_sum.109) | copy-start | bytes 18436
  2399.3 175.1 %copy-start.56 = (f32[256]{0:T(256)S(1)}, f32[256]{0:T(256)}, u32[]{:S(2)}) copy-start(f32[256]{0:T(256)} %convert_reduce_fusion.2) | copy-start | bytes 3076
  2561.1 85.3 %collective-permute-start.2 = (bf16[16,3584]{1,0:T(8,128)(2,1)S(1)}, bf16[16,3584]{1,0:T(8,128)(2,1)}, u32[]{:S(2)}, u32[]{:S(2)}) collective-permute-start(bf16[16,3584]{1,0:T(8,128)(2,1)S(1)} %get-tuple-element.30), channel_id=1, source_target_pairs={{0,3},{1,4},{2,5},{3,6},{4,7},{5,8},{6,9},{7,10},{8,11},{9,12},{10... | collective-permute-start | bytes 344072
  2566.6 82.2 %collective-permute-start.1 = (bf16[16,3584]{1,0:T(8,128)(2,1)S(1)}, bf16[16,3584]{1,0:T(8,128)(2,1)}, u32[]{:S(2)}, u32[]{:S(2)}) collective-permute-start(bf16[16,3584]{1,0:T(8,128)(2,1)S(1)} %get-tuple-element.30), channel_id=1, source_target_pairs={{0,2},{1,3},{2,4},{3,5},{4,6},{5,7},{6,8},{7,9},{8,10},{9,11},{10,... | collective-permute-start | bytes 344072
  2568.5 84.7 %collective-permute-start = (bf16[16,3584]{1,0:T(8,128)(2,1)S(1)}, bf16[16,3584]{1,0:T(8,128)(2,1)}, u32[]{:S(2)}, u32[]{:S(2)}) collective-permute-start(bf16[16,3584]{1,0:T(8,128)(2,1)S(1)} %get-tuple-element.30), channel_id=1, source_target_pairs={{0,1},{1,2},{2,3},{3,4},{4,5},{5,6},{6,7},{7,8},{8,9},{9,10},{10,1... | collective-permute-start | bytes 344072
  2571.2 72.1 %collective-permute-start.3 = (bf16[12,3584]{1,0:T(8,128)(2,1)S(1)}, bf16[12,3584]{1,0:T(8,128)(2,1)}, u32[]{:S(2)}, u32[]{:S(2)}) collective-permute-start(bf16[12,3584]{1,0:T(8,128)(2,1)S(1)} %slice.75), channel_id=1, source_target_pairs={{0,4},{1,5},{2,6},{3,7},{4,8},{5,9},{6,10},{7,11},{8,12},{9,13},{1... | collective-permute-start | bytes 258056
  2641.2 67.1 %collective-permute-start.6 = (bf16[16,26880]{1,0:T(8,128)(2,1)S(1)}, bf16[16,26880]{1,0:T(8,128)(2,1)S(1)}, u32[]{:S(2)}, u32[]{:S(2)}) collective-permute-start(bf16[16,26880]{1,0:T(8,128)(2,1)S(1)} %get-tuple-element.31), channel_id=1, source_target_pairs={{0,3},{1,4},{2,5},{3,6},{4,7},{5,8},{6,9},{7,10},{8,11},{9,12},{10... | collective-permute-start | bytes 2580488
  2643.4 64.9 %collective-permute-start.5 = (bf16[16,26880]{1,0:T(8,128)(2,1)S(1)}, bf16[16,26880]{1,0:T(8,128)(2,1)S(1)}, u32[]{:S(2)}, u32[]{:S(2)}) collective-permute-start(bf16[16,26880]{1,0:T(8,128)(2,1)S(1)} %get-tuple-element.31), channel_id=1, source_target_pairs={{0,2},{1,3},{2,4},{3,5},{4,6},{5,7},{6,8},{7,9},{8,10},{9,11},{10,... | collective-permute-start | bytes 2580488
  2646.3 62.0 %collective-permute-start.4 = (bf16[16,26880]{1,0:T(8,128)(2,1)S(1)}, bf16[16,26880]{1,0:T(8,128)(2,1)}, u32[]{:S(2)}, u32[]{:S(2)}) collective-permute-start(bf16[16,26880]{1,0:T(8,128)(2,1)S(1)} %get-tuple-element.31), channel_id=1, source_target_pairs={{0,1},{1,2},{2,3},{3,4},{4,5},{5,6},{6,7},{7,8},{8,9},{9,10},{10,1... | collective-permute-start | bytes 2580488
  2648.8 59.5 %collective-permute-start.7 = (bf16[12,26880]{1,0:T(8,128)(2,1)S(1)}, bf16[12,26880]{1,0:T(8,128)(2,1)}, u32[]{:S(2)}, u32[]{:S(2)}) collective-permute-start(bf16[12,26880]{1,0:T(8,128)(2,1)S(1)} %slice.76), channel_id=1, source_target_pairs={{0,4},{1,5},{2,6},{3,7},{4,8},{5,9},{6,10},{7,11},{8,12},{9,13},{1... | collective-permute-start | bytes 1935368
  (38 other events, 921.1 us)
Sparse Core Ops, SparseCore 0:
  9.7 204.1 all-gather.39
  215.6 200.0 all-gather.41
  417.5 242.3 all-gather.43
  661.5 237.8 all-gather.45
  901.0 238.0 all-gather.47
  1238.0 67.6 reduce-scatter.6
  1310.3 69.8 reduce-scatter.8
  1382.5 67.5 all-gather.21
  1452.9 65.2 all-gather.23
  1520.2 66.4 all-gather.27
  1589.0 62.3 all-gather.25
  1653.6 61.5 all-gather.29
  1717.5 198.8 all-gather.33
  1918.6 198.2 all-gather.31
  2119.0 60.9 all-gather.35
  2182.3 198.8 all-gather.37
where the time goes:
time: 2780 us; the launch traced here: 2770 us
  waiting for transfers between devices  1530 us (55%)
  blocking collectives  783 us (28%)
  local copies, waits for them, and re-layouts  211 us (8%)
  matrix products  175 us (6%)
    unnamed x2, blocking collectives  231 us
    all_gather x1, waiting for transfers between devices, per_device(): lax.all_gather(up_weight, ('ctx', 'fsdp'), axis=0, tiled=True)  204 us
    all_gather x1, waiting for transfers between devices, per_device(): lax.all_gather(grad_up, 'ctx', axis=0, tiled=True)  201 us
    all_gather x1, waiting for transfers between devices, per_device(): lax.all_gather(mixed_low, 'ctx', axis=0, tiled=True)  201 us
    unnamed x146, local copies, waits for them, and re-layouts  191 us
    all_gather x1, waiting for transfers between devices, per_device(): lax.all_gather(grad_gate, 'ctx', axis=0, tiled=True)  190 us
    all_gather x1, blocking collectives, per_device(): lax.all_gather(v_weight, ('ctx', 'fsdp'), axis=0, tiled=True)  189 us
    all_gather x1, blocking collectives, per_device(): lax.all_gather(k_weight, ('ctx', 'fsdp'), axis=0, tiled=True)  176 us
  transfers between devices with their start and end apart: 24, of which 15 were waited for; matrix products, arithmetic and copies ran while one was open for 9% of the time, Pallas kernels for 0%

commit v1 on v0

v1 whole, which is shorter than its diff:
```python
import math

import jax
import jax.numpy as jnp
from jax import lax
from jax.sharding import Mesh, PartitionSpec as P

H = 12
KVH = 2
HD = 128
GROUP = H // KVH
D = 1536
FF = 8960
BLK = 64
N_CTX = 8
ROWS = 12
PAD = 16
FFS = 1152
HALF_Q = GROUP * HD
QKV = HALF_Q + 2 * HD
MISC = 128
QKVM = QKV + MISC
FFW = 3 * FFS

epsilon = 1e-06
rope_base = 1000000.0

AXES = ("yh", "x", "z", "yl", "core")
Y = ("yh", "yl")
CTX = ("yh", "x")
TP = ("x", "core")
F32 = jnp.float32
BF = jnp.bfloat16
REL = (0, 3, 1, 2)


def shift(arr, axis, by):
    return lax.ppermute(arr, axis, [(i, (i + by) % 4) for i in range(4)])


def swap_core(arr):
    return lax.ppermute(arr, "core", [(0, 1), (1, 0)])


def ring_pieces(arr, axis):
    half = arr.shape[0] // 2
    prev = shift(arr, axis, 1)
    nxt = shift(arr, axis, 3)
    far_a = shift(prev[:half], axis, 1)
    far_b = shift(nxt[half:], axis, 3)
    return [arr, prev, nxt, jnp.concatenate([far_a, far_b], 0)]


def add_low(left, right):
    return (left.astype(F32) + right.astype(F32)).astype(BF)


def ring_reduce(pieces, axis):
    own, to_prev, to_next, far = pieces
    half = own.shape[0] // 2
    in_next = shift(far[:half], axis, 1)
    in_prev = shift(far[half:], axis, 3)
    to_next = jnp.concatenate([add_low(to_next[:half], in_next), to_next[half:]], 0)
    to_prev = jnp.concatenate([to_prev[:half], add_low(to_prev[half:], in_prev)], 0)
    from_prev = shift(to_next, axis, 1)
    from_next = shift(to_prev, axis, 3)
    return (own.astype(F32) + from_prev.astype(F32) + from_next.astype(F32)).astype(BF)


def gather_yz(block_a, block_b):
    first_a = jnp.concatenate(ring_pieces(block_a, "z"), 0)
    first_b = jnp.concatenate(ring_pieces(block_b, Y), 0)
    last_a = ring_pieces(first_a, Y)
    last_b = ring_pieces(first_b, "z")
    rows = block_b.shape[0]
    whole_a = jnp.concatenate(last_a, 0)
    whole_b = jnp.concatenate(
        [last_b[zr][yr * rows : (yr + 1) * rows] for yr in range(4) for zr in range(4)], 0
    )
    return whole_a, whole_b


def reduce_yz(whole_a, whole_b):
    rows = whole_b.shape[0] // 16
    first_a = [whole_a[4 * rows * p : 4 * rows * (p + 1)] for p in range(4)]
    first_b = [
        jnp.concatenate(
            [whole_b[(4 * yr + zr) * rows : (4 * yr + zr + 1) * rows] for yr in range(4)], 0
        )
        for zr in range(4)
    ]
    sum_a = ring_reduce(first_a, Y)
    sum_b = ring_reduce(first_b, "z")
    last_a = [sum_a[rows * p : rows * (p + 1)] for p in range(4)]
    last_b = [sum_b[rows * p : rows * (p + 1)] for p in range(4)]
    return ring_reduce(last_a, "z"), ring_reduce(last_b, Y)


def rope_tables(positions):
    half_dim = HD // 2
    frequency = jnp.exp(
        jnp.arange(half_dim, dtype=F32) * (-2.0 * math.log(rope_base) / HD)
    )
    angles = positions.astype(F32)[:, None] * frequency[None, :]
    cosine_tab = jnp.cos(angles)
    sine_tab = jnp.sin(angles)
    return (
        jnp.concatenate([cosine_tab, cosine_tab], -1),
        jnp.concatenate([sine_tab, sine_tab], -1),
    )


def rotate(values, cosine_tab, sine_tab):
    half_dim = values.shape[-1] // 2
    turned = jnp.concatenate([-values[..., half_dim:], values[..., :half_dim]], -1)
    return values * cosine_tab + turned * sine_tab


def unrotate(grads_in, cosine_tab, sine_tab):
    half_dim = grads_in.shape[-1] // 2
    scaled = grads_in * sine_tab
    return grads_in * cosine_tab + jnp.concatenate(
        [scaled[..., half_dim:], -scaled[..., :half_dim]], -1
    )


def product(left_arr, right_arr):
    return jnp.dot(left_arr, right_arr, preferred_element_type=F32)


def against(left_arr, right_arr):
    return lax.dot_general(
        left_arr, right_arr, (((1,), (1,)), ((), ())), preferred_element_type=F32
    )


def over_rows(left_arr, right_arr):
    return lax.dot_general(
        left_arr, right_arr, (((0,), (0,)), ((), ())), preferred_element_type=F32
    )


def per_device(
    tokens,
    cotangent,
    attn_gain,
    q_weight,
    q_bias,
    k_weight,
    k_bias,
    v_weight,
    v_bias,
    o_weight,
    mlp_gain,
    gate_weight,
    up_weight,
    down_weight,
):
    yh, x, z, yl, core = [lax.axis_index(a) for a in AXES]
    y = yh * 2 + yl
    ctx_rank = yh * 4 + x
    row_count = 2 * BLK
    score_scale = 1.0 / math.sqrt(HD)
    is_zero = core == 0

    place = jnp.arange(D, dtype=jnp.int32)
    rel = jnp.array(REL, jnp.int32)

    def rel_of(index):
        return jnp.where(index == 0, 0, jnp.where(index == 1, 3, index - 1))

    place_r = place % ROWS
    place_x = place // ROWS % 4
    place_c = place // (ROWS * 4) % 2
    place_z = (z + rel_of(place // (ROWS * 8) % 4)) % 4
    place_y = (y + rel_of(place // (ROWS * 32))) % 4
    place_dev = (((place_y // 2 * 4 + place_x) * 4 + place_z) * 2 + place_y % 2) * 2 + place_c
    natural = place_dev * ROWS + place_r
    to_order = (place[:, None] == natural[None, :]).astype(BF)

    def padded(arr):
        return jnp.pad(arr, ((0, PAD - ROWS), (0, 0)))

    misc = jnp.concatenate(
        [
            attn_gain[:, None],
            mlp_gain[:, None],
            q_bias[:, None],
            jnp.pad(k_bias[:, None], ((0, ROWS - 2), (0, 0))),
            jnp.pad(v_bias[:, None], ((0, ROWS - 2), (0, 0))),
            jnp.zeros((ROWS, MISC - 5), BF),
        ],
        1,
    )

    def side(h):
        return [
            q_weight[:, h * HALF_Q : (h + 1) * HALF_Q],
            k_weight[:, h * HD : (h + 1) * HD],
            v_weight[:, h * HD : (h + 1) * HD],
            misc,
            o_weight[:, h * HALF_Q : (h + 1) * HALF_Q],
        ]

    attn_pack = padded(jnp.concatenate(side(0) + side(1), 1))
    side_width = QKVM + HALF_Q
    along_x = jnp.concatenate(
        [attn_pack, shift(attn_pack, "x", 1), shift(attn_pack, "x", 3), shift(attn_pack, "x", 2)],
        0,
    )
    left_side, right_side = along_x[:, :side_width], along_x[:, side_width:]
    keep_side = jnp.where(is_zero, left_side, right_side)
    send_side = jnp.where(is_zero, right_side, left_side)
    both_rows = jnp.concatenate([keep_side, swap_core(send_side)], 0)
    want = jnp.arange(8 * ROWS, dtype=jnp.int32)
    want_c = want // (4 * ROWS)
    want_x = want // ROWS % 4
    x_off = (want_x - x) % 4
    x_rel = jnp.where(x_off == 0, 0, jnp.where(x_off == 3, 1, x_off + 1))
    at = ((want_c ^ core) * 4 + x_rel) * PAD + want % ROWS
    pick = (at[:, None] == jnp.arange(8 * PAD, dtype=jnp.int32)[None, :]).astype(BF)
    attn_rows = product(pick, both_rows).astype(BF)
    cut_q, cut_o = 5 * HD, 3 * HD
    qkv_a, qkv_b = gather_yz(attn_rows[:, :cut_q], attn_rows[:, cut_q:QKVM])
    qkvm_own = jnp.concatenate([qkv_a, qkv_b], 1)
    weight_own = qkvm_own[:, :QKV]
    weight_sib = swap_core(weight_own)
    o_a, o_b = gather_yz(
        attn_rows[:, QKVM : QKVM + cut_o], attn_rows[:, QKVM + cut_o :]
    )
    o_own = jnp.concatenate([o_a, o_b], 1)
    o_sib = swap_core(o_own)

    def ff_padded(arr):
        return jnp.pad(arr, ((0, PAD - ROWS), (0, 8 * FFS - FF)))

    ff_arrs = [ff_padded(a) for a in (gate_weight, up_weight, down_weight)]
    ff_send = jnp.stack(
        [
            jnp.concatenate([a[:, t * FFS : (t + 1) * FFS] for a in ff_arrs], 1)
            for t in range(8)
        ]
    )
    ff_got = lax.all_to_all(ff_send, TP, split_axis=0, concat_axis=0, tiled=True)
    ff_at = (want_x * 2 + want_c) * PAD + want % ROWS
    ff_pick = (ff_at[:, None] == jnp.arange(8 * PAD, dtype=jnp.int32)[None, :]).astype(BF)
    ff_rows = product(ff_pick, ff_got.reshape(8 * PAD, FFW)).astype(BF)
    cut_f = 14 * HD
    ff_a, ff_b = gather_yz(ff_rows[:, :cut_f], ff_rows[:, cut_f:])
    ff_all = jnp.concatenate([ff_a, ff_b], 1)
    weight_gate = ff_all[:, :FFS]
    weight_up = ff_all[:, FFS : 2 * FFS]
    weight_down = ff_all[:, 2 * FFS :]

    misc_rows = against(
        (jnp.arange(8)[:, None] == jnp.arange(MISC)[None, :]).astype(BF), qkvm_own[:, QKV:]
    )
    gain_one = misc_rows[0:1]
    gain_two = misc_rows[1:2]
    bias_rows = misc_rows.astype(BF)
    bias_q = against(bias_rows[2:3], to_order).reshape(2, HALF_Q)
    small = jnp.arange(KVH * HD, dtype=jnp.int32)
    to_small = (
        (place_dev * 2 + place_r)[:, None] == small[None, :]
    ) & (place_r < 2)[:, None]
    bias_kv = product(bias_rows[3:5], to_small.astype(BF))
    bias_k = bias_kv[0].reshape(2, HD)
    bias_v = bias_kv[1].reshape(2, HD)

    def sided(pair):
        return jnp.where(is_zero, pair, pair[::-1])

    bias_q, bias_k, bias_v = sided(bias_q), sided(bias_k), sided(bias_v)

    offsets = jnp.arange(BLK, dtype=jnp.int32)
    query_pos = jnp.concatenate(
        [ctx_rank * BLK + offsets, (2 * N_CTX - 1 - ctx_rank) * BLK + offsets]
    )
    sources = ctx_rank ^ jnp.arange(N_CTX, dtype=jnp.int32)
    key_pos = jnp.stack(
        [
            sources[:, None] * BLK + offsets[None, :],
            (2 * N_CTX - 1 - sources)[:, None] * BLK + offsets[None, :],
        ],
        1,
    ).reshape(-1)
    visible = query_pos[:, None] >= key_pos[None, :]
    cosine_tab, sine_tab = rope_tables(query_pos)
    cosine_b = cosine_tab[:, None, :]
    sine_b = sine_tab[:, None, :]

    inputs_low = product(tokens.reshape(row_count, D), to_order).astype(BF)
    grad_low = product(cotangent.reshape(row_count, D), to_order).astype(BF)
    inputs = inputs_low.astype(F32)
    grad_out = grad_low.astype(F32)
    grad_rows = lax.all_gather(grad_low, TP, axis=0, tiled=True)

    scale_one = lax.rsqrt(jnp.mean(inputs * inputs, axis=-1, keepdims=True) + epsilon)
    unit_one = inputs * scale_one
    normed_one = (unit_one * gain_one).astype(BF)
    lin = [product(normed_one, weight_own), product(normed_one, weight_sib)]
    query_lin = jnp.stack([lin[s][:, :HALF_Q] + bias_q[s] for s in range(2)], 1)
    key_lin = jnp.stack([lin[s][:, HALF_Q : HALF_Q + HD] + bias_k[s] for s in range(2)], 1)
    value_low = jnp.stack([lin[s][:, HALF_Q + HD :] + bias_v[s] for s in range(2)], 1).astype(BF)
    query_rot = rotate(
        query_lin.reshape(row_count, H, HD), cosine_b, sine_b
    ).astype(BF).reshape(row_count, KVH, GROUP, HD)
    key_rot = rotate(key_lin, cosine_b, sine_b).astype(BF)
    kv_send = jnp.concatenate(
        [key_rot.reshape(row_count, KVH * HD), value_low.reshape(row_count, KVH * HD)], 1
    )

    def to_ctx(arr, k):
        return lax.ppermute(arr, CTX, [(i, i ^ k) for i in range(N_CTX)])

    kv_all = jnp.concatenate([kv_send] + [to_ctx(kv_send, k) for k in range(1, N_CTX)], 0)
    key_heads = kv_all[:, : KVH * HD].reshape(N_CTX * row_count, KVH, HD)
    value_heads = kv_all[:, KVH * HD :].reshape(N_CTX * row_count, KVH, HD)
    scores = (
        jnp.einsum("lkrd,mkd->krlm", query_rot, key_heads, preferred_element_type=F32)
        * score_scale
    )
    masked = jnp.where(visible, scores, -jnp.inf)
    row_max = jnp.max(masked, axis=-1, keepdims=True)
    exp_terms = jnp.exp(masked - row_max)
    row_sum = jnp.sum(exp_terms, axis=-1, keepdims=True)
    probs = exp_terms / row_sum
    probs_low = probs.astype(BF)
    context = jnp.einsum("krlm,mkd->lkrd", probs_low, value_heads, preferred_element_type=F32)
    context_low = context.reshape(row_count, H * HD).astype(BF)
    hidden_one = (
        inputs
        + against(context_low[:, :HALF_Q], o_own)
        + against(context_low[:, HALF_Q:], o_sib)
    )
    scale_two = lax.rsqrt(jnp.mean(hidden_one * hidden_one, axis=-1, keepdims=True) + epsilon)
    unit_two = hidden_one * scale_two
    normed_two = (unit_two * gain_two).astype(BF)

    normed_rows = lax.all_gather(normed_two, TP, axis=0, tiled=True)
    grad_mixed = product(grad_rows, weight_down)
    gate_val = product(normed_rows, weight_gate)
    up_val = product(normed_rows, weight_up)
    gate_sig = jax.nn.sigmoid(gate_val)
    swish = gate_val * gate_sig
    mixed_low = (swish * up_val).astype(BF)
    grad_up = (grad_mixed * swish).astype(BF)
    grad_gate = (grad_mixed * up_val * gate_sig * (1.0 + gate_val * (1.0 - gate_sig))).astype(BF)
    grad_norm_part = (against(grad_gate, weight_gate) + against(grad_up, weight_up)).astype(BF)
    grad_norm_two = lax.psum_scatter(
        grad_norm_part, TP, scatter_dimension=0, tiled=True
    ).astype(F32)
    down_part = against(mixed_low, weight_down).astype(BF)
    down_terms = lax.psum_scatter(down_part, TP, scatter_dimension=0, tiled=True)
    layer_sum = (hidden_one + down_terms.astype(F32)).astype(BF)
    layer_out = against(layer_sum, to_order).astype(BF).reshape(tokens.shape)
    ff_grads = jnp.concatenate(
        [
            over_rows(normed_rows, grad_gate).astype(BF),
            over_rows(normed_rows, grad_up).astype(BF),
            over_rows(grad_rows, mixed_low).astype(BF),
        ],
        1,
    )
    ff_sum_a, ff_sum_b = reduce_yz(ff_grads[:, :cut_f], ff_grads[:, cut_f:])
    ff_sum = jnp.concatenate([ff_sum_a, ff_sum_b], 1)
    ff_back = lax.dot_general(
        ff_pick, ff_sum, (((0,), (0,)), ((), ())), preferred_element_type=F32
    ).astype(BF)
    ff_back = lax.all_to_all(
        ff_back.reshape(8, PAD, FFW), TP, split_axis=0, concat_axis=0, tiled=True
    )
    gate_weight_grad, up_weight_grad, down_weight_grad = [
        jnp.concatenate(
            [ff_back[t, :ROWS, i * FFS : (i + 1) * FFS] for t in range(8)], 1
        )[:, :FF].astype(F32)
        for i in range(3)
    ]

    gain_two_term = jnp.sum(grad_norm_two * unit_two, axis=0)
    grad_unit_two = grad_norm_two * gain_two
    grad_hidden = grad_out + scale_two * (
        grad_unit_two - unit_two * jnp.mean(grad_unit_two * unit_two, axis=-1, keepdims=True)
    )
    grad_branch = grad_hidden.astype(BF)
    grad_context = jnp.concatenate(
        [product(grad_branch, o_own), product(grad_branch, o_sib)], 1
    ).astype(BF)
    grad_ctx_heads = grad_context.reshape(row_count, KVH, GROUP, HD)
    grad_probs = jnp.einsum(
        "lkrd,mkd->krlm", grad_ctx_heads, value_heads, preferred_element_type=F32
    )
    row_delta = jnp.sum(probs * grad_probs, axis=-1, keepdims=True)
    grad_scores = (probs * (grad_probs - row_delta)).astype(BF)
    grad_query = (
        jnp.einsum("krlm,mkd->lkrd", grad_scores, key_heads, preferred_element_type=F32)
        * score_scale
    )
    grad_key_all = (
        jnp.einsum("krlm,lkrd->mkd", grad_scores, query_rot, preferred_element_type=F32)
        * score_scale
    )
    grad_value_all = jnp.einsum(
        "krlm,lkrd->mkd", probs_low, grad_ctx_heads, preferred_element_type=F32
    )
    grad_kv = jnp.concatenate(
        [
            grad_key_all.reshape(N_CTX * row_count, KVH * HD),
            grad_value_all.reshape(N_CTX * row_count, KVH * HD),
        ],
        1,
    ).astype(BF)
    grad_kv_sum = grad_kv[:row_count].astype(F32)
    for k in range(1, N_CTX):
        grad_kv_sum = grad_kv_sum + to_ctx(
            grad_kv[k * row_count : (k + 1) * row_count], k
        ).astype(F32)
    grad_key = grad_kv_sum[:, : KVH * HD].reshape(row_count, KVH, HD)
    grad_q_lin = unrotate(grad_query.reshape(row_count, H, HD), cosine_b, sine_b).astype(BF)
    grad_q_lin = grad_q_lin.reshape(row_count, KVH, HALF_Q)
    grad_k_lin = unrotate(grad_key, cosine_b, sine_b).astype(BF)
    grad_v_lin = grad_kv_sum[:, KVH * HD :].astype(BF).reshape(row_count, KVH, HD)
    grad_lin = [
        jnp.concatenate([grad_q_lin[:, s], grad_k_lin[:, s], grad_v_lin[:, s]], 1)
        for s in range(2)
    ]
    grad_norm_one = against(grad_lin[0], weight_own) + against(grad_lin[1], weight_sib)
    gain_one_term = jnp.sum(grad_norm_one * unit_one, axis=0)
    grad_unit_one = grad_norm_one * gain_one
    input_grad = grad_hidden + scale_one * (
        grad_unit_one - unit_one * jnp.mean(grad_unit_one * unit_one, axis=-1, keepdims=True)
    )
    input_high = input_grad.astype(BF)
    input_rest = (input_grad - input_high.astype(F32)).astype(BF)
    input_grad = (against(input_high, to_order) + against(input_rest, to_order)).reshape(
        tokens.shape
    )

    def unsided(pair):
        return jnp.where(is_zero, pair, pair[::-1])

    q_bias_term = unsided(jnp.sum(grad_q_lin.astype(F32), axis=0)).reshape(1, D)
    k_bias_term = unsided(jnp.sum(grad_k_lin.astype(F32), axis=0)).reshape(1, KVH * HD)
    v_bias_term = unsided(jnp.sum(grad_v_lin.astype(F32), axis=0)).reshape(1, KVH * HD)
    k_bias_grad = jnp.pad(k_bias_term, ((0, 7), (0, 0)))
    k_bias_grad = k_bias_grad + swap_core(k_bias_grad)
    for axis in ("x", Y, "z"):
        for k in (1, 2):
            k_bias_grad = k_bias_grad + lax.ppermute(
                k_bias_grad, axis, [(i, i ^ k) for i in range(4)]
            )
    k_bias_grad = k_bias_grad[0]
    q_bias_ordered = product(q_bias_term.astype(BF), to_order)
    v_bias_ordered = against(v_bias_term.astype(BF), to_small.astype(BF))
    terms = jnp.concatenate(
        [
            gain_one_term[None],
            gain_two_term[None],
            q_bias_ordered,
            jnp.zeros((1, D), F32),
            v_bias_ordered,
            jnp.zeros((3, D), F32),
        ],
        0,
    ).astype(BF)
    misc_grad = over_rows(
        terms, (jnp.arange(8)[:, None] == jnp.arange(MISC)[None, :]).astype(BF)
    ).astype(BF)

    def to_owners(own, sib, cut):
        total = add_low(own, swap_core(sib))
        part_a, part_b = reduce_yz(total[:, :cut], total[:, cut:])
        part = jnp.concatenate([part_a, part_b], 1)
        spread_at = (place_spread := jnp.arange(8 * PAD, dtype=jnp.int32))
        sp_xr = place_spread // (2 * PAD)
        sp_c = place_spread // PAD % 2
        sp_r = place_spread % PAD
        sp_x = (x + jnp.where(sp_xr == 0, 0, jnp.where(sp_xr == 1, 3, sp_xr - 1))) % 4
        source = jnp.where(sp_r < ROWS, (sp_c * 4 + sp_x) * ROWS + sp_r, -1)
        spread = (source[:, None] == jnp.arange(8 * ROWS)[None, :]).astype(BF)
        spaced = product(spread, part).astype(BF)
        two = 2 * PAD
        mine = spaced[:two].astype(F32)
        mine = mine + shift(spaced[two : 2 * two], "x", 3).astype(F32)
        mine = mine + shift(spaced[2 * two : 3 * two], "x", 1).astype(F32)
        mine = mine + shift(spaced[3 * two :], "x", 2).astype(F32)
        mine = mine.astype(BF)
        keep = jnp.where(is_zero, mine[:PAD], mine[PAD:])
        give = jnp.where(is_zero, mine[PAD:], mine[:PAD])
        got = swap_core(give)
        side0 = jnp.where(is_zero, keep, got)[:ROWS].astype(F32)
        side1 = jnp.where(is_zero, got, keep)[:ROWS].astype(F32)
        return side0, side1

    o_grads = to_owners(
        over_rows(grad_branch, context_low[:, :HALF_Q]).astype(BF),
        over_rows(grad_branch, context_low[:, HALF_Q:]).astype(BF),
        cut_o,
    )
    o_weight_grad = jnp.concatenate(o_grads, 1)
    qkvm_grads = to_owners(
        jnp.concatenate([over_rows(normed_one, grad_lin[0]).astype(BF), misc_grad], 1),
        jnp.concatenate([over_rows(normed_one, grad_lin[1]).astype(BF), misc_grad], 1),
        cut_q,
    )
    q_weight_grad = jnp.concatenate([g[:, :HALF_Q] for g in qkvm_grads], 1)
    k_weight_grad = jnp.concatenate([g[:, HALF_Q : HALF_Q + HD] for g in qkvm_grads], 1)
    v_weight_grad = jnp.concatenate([g[:, HALF_Q + HD : QKV] for g in qkvm_grads], 1)
    misc_mine = qkvm_grads[0][:, QKV:]
    attn_gain_grad = misc_mine[:, 0]
    mlp_gain_grad = misc_mine[:, 1]
    q_bias_grad = misc_mine[:, 2]
    v_bias_grad = misc_mine[:2, 4]
    return (
        layer_out,
        input_grad,
        attn_gain_grad,
        q_weight_grad,
        q_bias_grad,
        k_weight_grad,
        k_bias_grad,
        v_weight_grad,
        v_bias_grad,
        o_weight_grad,
        mlp_gain_grad,
        gate_weight_grad,
        up_weight_grad,
        down_weight_grad,
    )


def solution(mesh):
    fine = Mesh(mesh.devices.reshape(2, 4, 4, 2, 2), AXES)
    acts = P(("z", "yl", "core"), None, CTX, None)
    vec, mat = P(AXES), P(AXES, None)
    return jax.shard_map(
        per_device,
        mesh=fine,
        in_specs=(acts, acts, vec, mat, vec, mat, vec, mat, vec, mat, vec, mat, mat, mat),
        out_specs=(acts, acts, vec, mat, vec, mat, P(), mat, vec, mat, vec, mat, mat, mat),
        check_vma=False,
    )
```

time: 2780 us -> 727 us (0.26)
  waiting for transfers between devices: 1530 us -> 110 us
  blocking collectives: 783 us -> 0 us
  starting transfers between devices: 25.9 us -> 232 us
  local copies, waits for them, and re-layouts: 211 us -> 143 us
  other arithmetic: 26.9 us -> 84.4 us
  matrix products: 175 us -> 128 us
    all_gather x14 -> x2, waiting for transfers between devices: 1390 us -> 4.84 us  [the longest x1 4.84 us: per_device(): normed_rows = lax.all_gather(normed_two, TP, axis=0, tiled=True)]
    all_gather x6 -> x0, blocking collectives: 488 us -> none  [the longest x1 189 us: per_device(): lax.all_gather(v_weight, ('ctx', 'fsdp'), axis=0, tiled=True)]
    unnamed x2 -> x0, blocking collectives: 231 us -> none
    ppermute x0 -> x133, starting transfers between devices: none -> 217 us  [the longest x105 141 us: shift(): return lax.ppermute(arr, axis, [(i, (i + by) % 4) for i in range(4)])]
    unnamed x146 -> x389, local copies, waits for them, and re-layouts: 191 us -> 70.5 us
    ppermute x0 -> x133, waiting for transfers between devices: none -> 101 us  [the longest x105 77.8 us: shift(): return lax.ppermute(arr, axis, [(i, (i + by) % 4) for i in range(4)])]
    reduce_scatter x2 -> x0, waiting for transfers between devices: 92.6 us -> none  [the longest x1 67.9 us: per_device(): lax.psum_scatter(grad_value_all.reshape(seqs_here, 2, n_ctx * block_len,...]
    psum x1 -> x0, blocking collectives: 64.2 us -> none  [per_device(): lax.psum((gain_one_term, q_bias_term, k_bias_term, v_bias_term, gain_two_...]
  transfers between devices with their start and end apart: 24 -> 139, of which waited for: 15 -> 46; matrix products, arithmetic and copies ran while one was open for 9% -> 42% of each run, Pallas kernels for 0% -> 0%
where the time goes in v1:
time: 727 us; the launch traced here: 714 us
  starting transfers between devices  232 us (32%)
  local copies, waits for them, and re-layouts  143 us (20%)
  matrix products  128 us (18%)
  waiting for transfers between devices  110 us (15%)
  other arithmetic  84.4 us (12%)
  between operations  17.2 us (2%)
    ppermute x105, starting transfers between devices, shift(): return lax.ppermute(arr, axis, [(i, (i + by) % 4) for i in range(4)])  141 us
    ppermute x105, waiting for transfers between devices, shift(): return lax.ppermute(arr, axis, [(i, (i + by) % 4) for i in range(4)])  77.8 us
    unnamed x389, local copies, waits for them, and re-layouts  70.5 us
    ppermute x8, starting transfers between devices, swap_core(): return lax.ppermute(arr, 'core', [(0, 1), (1, 0)])  44.5 us
    dot_general x13, matrix products, against(): lax.dot_general(left_arr, right_arr, (((1,), (1,)), ((), ())), preferred_...  44.2 us
    dot_general x15, matrix products, product(): return jnp.dot(left_arr, right_arr, preferred_element_type=F32)  38.8 us
    dot_general x8, matrix products, over_rows(): lax.dot_general(left_arr, right_arr, (((0,), (0,)), ((), ())), preferred_...  25.4 us
    ppermute x14, starting transfers between devices, to_ctx(): return lax.ppermute(arr, CTX, [(i, i ^ k) for i in range(N_CTX)])  21.1 us
  transfers between devices with their start and end apart: 139, of which 46 were waited for; matrix products, arithmetic and copies ran while one was open for 42% of the time, Pallas kernels for 0%

profile of v1, /device:TPU:1, one launch (start us, length us, event | category | flops | bytes accessed | tf_op | source)
XLA Modules:
  0.0 713.8 jit_solution(15389600117242126470)
XLA Ops:
  26.5 5.0 all-to-all-start
  76.9 3.6 collective-permute-done.14
  81.3 3.4 collective-permute-done.15
  102.9 3.1 collective-permute-done.42
  106.2 4.1 collective-permute-done.43
  134.9 12.2 %collective-permute-start.55 = (bf16[48,1664]{1,0:T(8,128)(2,1)}, bf16[48,1664]{1,0:T(8,128)(2,1)S(1)}, u32[]{:S(2)}, u32[]{:S(2)}) collective-permute-start(bf16[48,1664]{1,0:T(8,128)(2,1)} %slice.1539), channel_id=1, source_target_pairs={{0,2},{2,64},{64,66},{66,0},{1,3},{3,65},{65,67},{67,1},{4,6},{6,6... | collective-permute-start | bytes 479240 | tf_op jit(solution)/shard_map/ppermute | solution.py:38
  173.7 16.3 %collective-permute-start.20 = (bf16[1536,1024]{1,0:T(8,128)(2,1)S(1)}, bf16[1536,1024]{1,0:T(8,128)(2,1)}, u32[]{:S(2)}, u32[]{:S(2)}) collective-permute-start(bf16[1536,1024]{1,0:T(8,128)(2,1)S(1)} %pad_maximum_fusion.3), channel_id=1, source_target_pairs={{0,1},{1,0},{2,3},{3,2},{4,5},{5,4},{6,7},{7,6},{8,9},{9,8},{10,11... | collective-permute-start | bytes 9437192 | tf_op jit(solution)/shard_map/ppermute | solution.py:42
  243.1 3.2 collective-permute-done.25
  247.2 3.8 collective-permute-done.26
  254.7 4.7 fusion.287
  259.5 3.4 fusion.113
  286.8 9.6 %fusion.28 = f32[1024,1152]{1,0:T(8,128)} fusion(bf16[1024,1536]{0,1:T(8,128)(2,1)} %all-gather.5.cloned.1.call-done, bf16[1536,1664]{1,0:T(8,128)(2,1)} %slice_dynamic-update-slice_fusion), kind=kOutput, calls=%fused_computation.69 | convolution fusion | flops 3623878656 | bytes 11403264 | tf_op jit(solution)/shard_map/dot_general | solution.py:128
  296.4 4.8 all-gather.3.cloned.1.call-done
  301.3 7.6 %fusion.259 = f32[1024,1152]{1,0:T(8,128)S(1)} fusion(bf16[1024,1536]{0,1:T(8,128)(2,1)} %all-gather.3.cloned.1.call-done, bf16[1536,1664]{1,0:T(8,128)(2,1)} %slice_dynamic-update-slice_fusion, bf16[1536,1792]{1,0:T(8,128)(2,1)} %constant_dynamic-update-slice_fusion.93), kind=kOutput, calls=%fused_computation.770 | convolution fusion | flops 3630956544 | bytes 18481152 | tf_op jit(solution)/shard_map/dot_general | solution.py:128
  308.9 7.7 %multiply_convert_fusion.1 = (bf16[1024,1152]{1,0:T(8,128)(2,1)S(1)}, bf16[1024,1152]{1,0:T(8,128)(2,1)S(1)}, bf16[1024,1152]{1,0:T(8,128)(2,1)}) fusion(f32[1024,1152]{1,0:T(8,128)S(1)} %copy-done.139, f32[1024,1152]{1,0:T(8,128)S(1)} %fusion.259, bf16[1024,1536]{0,1:T(8,128)(2,1)S(1)} %copy-done.137, bf16[1536,1792]{1,0:T(8,128)(2,1)S(1)} %copy-done.112), kind=kOutput, calls=%fused_computation.39 | convolution fusion | flops 3641573376 | bytes 23199744 | tf_op jit(solution)/shard_map/dot_general | solution.py:128
  316.6 4.3 convolution_convert_fusion.2
  320.9 4.3 convolution_convert_fusion.1
  325.2 6.1 fusion.124
  338.6 6.5 convolution_convert_fusion
  356.9 9.6 %fusion.260 = f32[1024,1536]{1,0:T(8,128)} fusion(bf16[1024,1152]{1,0:T(8,128)(2,1)} %copy-done.140, bf16[1536,1664]{1,0:T(8,128)(2,1)} %slice_dynamic-update-slice_fusion, bf16[1536,1792]{1,0:T(8,128)(2,1)} %constant_dynamic-update-slice_fusion.93), kind=kOutput, calls=%fused_computation.771 | convolution fusion | flops 3630956544 | bytes 19267584 | tf_op jit(solution)/shard_map/dot_general | solution.py:132
  372.9 3.7 add_convert_fusion.8
  376.6 9.5 %fusion.105 = (bf16[384,1664]{0,1:T(8,128)(2,1)}, bf16[384,1664]{0,1:T(8,128)(2,1)}) fusion(bf16[1536,1152]{0,1:T(8,128)(2,1)S(1)} %copy-done.3, bf16[1536,1152]{0,1:T(8,128)(2,1)S(1)} %convolution_convert_fusion.1, bf16[192,1664]{0,1:T(8,128)(2,1)S(1)} %get-tuple-element.42, bf16[192,1664]{0,1:T(8,128)(2,1)S(1)} %get-tuple-element.43), kind=kLoop, calls=%fused_computation.165 | loop fusion | flops 23003136 | bytes 10911744 | tf_op jit(solution)/shard_map/concatenate | solution.py:63
  388.9 5.8 add_convert_fusion.1
  405.8 9.3 %collective-permute-done.126 = bf16[384,1664]{0,1:T(8,128)(2,1)} collective-permute-done((bf16[384,1664]{0,1:T(8,128)(2,1)}, bf16[384,1664]{0,1:T(8,128)(2,1)}, u32[]{:S(2)}, u32[]{:S(2)}) %collective-permute-start.126) | collective-permute-done | bytes 1277984 | tf_op jit(solution)/shard_map/ppermute | solution.py:38
  415.2 11.0 %add_convert_fusion.4 = bf16[384,1664]{0,1:T(8,128)(2,1)S(1)} fusion(bf16[384,1664]{0,1:T(8,128)(2,1)} %collective-permute-done.128, bf16[384,1664]{0,1:T(8,128)(2,1)} %collective-permute-done.126, bf16[1536,1152]{0,1:T(8,128)(2,1)S(1)} %copy-done.4, bf16[1536,1152]{0,1:T(8,128)(2,1)S(1)} %convolution_convert_fusion.1), kind=kLoop, calls=%fused_computation.86 | loop fusion | flops 23642112 | bytes 10911744 | tf_op jit(solution)/shard_map/convert_element_type | solution.py:67
  429.4 3.4 collective-permute-done.118
  436.8 5.2 collective-permute-done.129
  452.2 3.4 collective-permute-done.122
  457.3 9.4 %all-to-all-start.1 = ((bf16[8,16,3456]{2,1,0:T(8,128)(2,1)}), bf16[8,16,3456]{2,1,0:T(8,128)(2,1)S(1)}, u32[]{:S(2)}, u32[]{:S(2)}) async-start(bf16[8,16,3456]{2,1,0:T(8,128)(2,1)} %bitcast.86), calls=%async_computation.1 | async-start | bytes 1769472 | tf_op jit(solution)/shard_map/all_to_all | solution.py:370
  467.1 8.7 %convolution_convert_fusion.7 = bf16[1024,1536]{1,0:T(8,128)(2,1)} fusion(bf16[1024,1152]{1,0:T(8,128)(2,1)} %get-tuple-element.33, bf16[1536,1664]{1,0:T(8,128)(2,1)} %slice_dynamic-update-slice_fusion), kind=kOutput, calls=%fused_computation.60 | convolution fusion | flops 3625451520 | bytes 9043968 | tf_op jit(solution)/shard_map/dot_general | solution.py:132
  475.8 4.2 all-to-all-done.1
  495.6 4.0 fusion.12
  499.5 3.8 fusion.14
  504.6 4.1 fusion.93
  518.4 3.0 rev.21
  523.7 3.1 convolution_convert_fusion.8
  534.7 4.4 collective-permute-start.66
  555.1 3.0 fusion.189
  567.7 3.1 collective-permute-start.89
  579.1 3.2 collective-permute-start.92
  588.9 3.0 fusion.44
  591.9 3.0 collective-permute-start.95
  607.6 4.3 collective-permute-done.98
  648.0 3.2 collective-permute-start.80
  659.2 15.4 %collective-permute-start.116 = (bf16[16,768]{1,0:T(8,128)(2,1)S(1)}, bf16[16,768]{1,0:T(8,128)(2,1)S(1)}, u32[]{:S(2)}, u32[]{:S(2)}) collective-permute-start(bf16[16,768]{1,0:T(8,128)(2,1)S(1)} %get-tuple-element.263), channel_id=1, source_target_pairs={{0,1},{1,0},{2,3},{3,2},{4,5},{5,4},{6,7},{7,6},{8,9},{9,8},{10,11... | collective-permute-start | bytes 73736 | tf_op jit(solution)/shard_map/ppermute | solution.py:42
  675.7 3.5 collective-permute-start.75
  692.4 3.8 collective-permute-done.86
  696.2 6.6 collective-permute-start.88
  (940 shorter events, 425.0 us)
Async XLA Ops:
  14.1 24.0 %collective-permute-start = (bf16[16,3840]{1,0:T(8,128)(2,1)S(1)}, bf16[16,3840]{1,0:T(8,128)(2,1)S(1)}, u32[]{:S(2)}, u32[]{:S(2)}) collective-permute-start(bf16[16,3840]{1,0:T(8,128)(2,1)S(1)} %pad.27), channel_id=1, source_target_pairs={{0,16},{16,32},{32,48},{48,0},{1,17},{17,33},{33,49},{49,1},{2,18}... | collective-permute-start | bytes 368648 | tf_op jit(solution)/shard_map/ppermute | solution.py:38
  16.2 21.9 %collective-permute-start.1 = (bf16[16,3840]{1,0:T(8,128)(2,1)S(1)}, bf16[16,3840]{1,0:T(8,128)(2,1)S(1)}, u32[]{:S(2)}, u32[]{:S(2)}) collective-permute-start(bf16[16,3840]{1,0:T(8,128)(2,1)S(1)} %pad.27), channel_id=1, source_target_pairs={{0,48},{16,0},{32,16},{48,32},{1,49},{17,1},{33,17},{49,33},{2,50}... | collective-permute-start | bytes 368648 | tf_op jit(solution)/shard_map/ppermute | solution.py:38
  17.6 20.5 %collective-permute-start.2 = (bf16[16,3840]{1,0:T(8,128)(2,1)S(1)}, bf16[16,3840]{1,0:T(8,128)(2,1)S(1)}, u32[]{:S(2)}, u32[]{:S(2)}) collective-permute-start(bf16[16,3840]{1,0:T(8,128)(2,1)S(1)} %pad.27), channel_id=1, source_target_pairs={{0,32},{16,48},{32,0},{48,16},{1,33},{17,49},{33,1},{49,17},{2,34}... | collective-permute-start | bytes 368648 | tf_op jit(solution)/shard_map/ppermute | solution.py:38
  26.5 68.1 %all-to-all-start = ((bf16[8,16,3456]{2,1,0:T(8,128)(2,1)}), bf16[8,16,3456]{2,1,0:T(8,128)(2,1)S(1)}, u32[]{:S(2)}, u32[]{:S(2)}) async-start(bf16[8,16,3456]{2,1,0:T(8,128)(2,1)} %constant_dynamic-update-slice_fusion.80), calls=%async_computation | async-start | bytes 1769472 | tf_op jit(solution)/shard_map/all_to_all | solution.py:244
  31.5 255.3 %all-gather.5.cloned.1.call-start = ((), (), s32[]{:S(2)}) async-start(), calls=%async_computation.5 | async-start | bytes 3538944 | tf_op jit(solution)/shard_map/all_gather | solution.py:296
  33.8 267.5 %all-gather.3.cloned.1.call-start = ((), (), s32[]{:S(2)}) async-start(), calls=%async_computation.4 | async-start | bytes 3538944 | tf_op jit(solution)/shard_map/all_gather | solution.py:340
  51.8 20.3 %collective-permute-start.13 = (bf16[96,640]{1,0:T(8,128)(2,1)S(1)}, bf16[96,640]{1,0:T(8,128)(2,1)S(1)}, u32[]{:S(2)}, u32[]{:S(2)}) collective-permute-start(bf16[96,640]{1,0:T(8,128)(2,1)S(1)} %get-tuple-element.167), channel_id=1, source_target_pairs={{0,12},{4,0},{8,4},{12,8},{1,13},{5,1},{9,5},{13,9},{2,14},{6,2},{... | collective-permute-start | bytes 368648 | tf_op jit(solution)/shard_map/ppermute | solution.py:38
  68.7 19.9 %collective-permute-start.33 = (bf16[384,384]{1,0:T(8,128)(2,1)S(1)}, bf16[384,384]{1,0:T(8,128)(2,1)S(1)}, u32[]{:S(2)}, u32[]{:S(2)}) collective-permute-start(bf16[384,384]{1,0:T(8,128)(2,1)S(1)} %get-tuple-element.268), channel_id=1, source_target_pairs={{0,66},{2,0},{64,2},{66,64},{1,67},{3,1},{65,3},{67,65},{4,70},{6,... | collective-permute-start | bytes 884744 | tf_op jit(solution)/shard_map/ppermute | solution.py:38
  72.9 19.8 %collective-permute-start.41 = (bf16[384,384]{1,0:T(8,128)(2,1)S(1)}, bf16[384,384]{1,0:T(8,128)(2,1)S(1)}, u32[]{:S(2)}, u32[]{:S(2)}) collective-permute-start(bf16[384,384]{1,0:T(8,128)(2,1)S(1)} %constant_dynamic-update-slice_fusion.14), channel_id=1, source_target_pairs={{0,12},{4,0},{8,4},{12,8},{1,13},{5,1},{9,5},{13,9},{2,14},{6,2},{... | collective-permute-start | bytes 884744 | tf_op jit(solution)/shard_map/ppermute | solution.py:38
  88.7 27.6 %collective-permute-start.16 = (bf16[384,640]{1,0:T(8,128)(2,1)}, bf16[384,640]{1,0:T(8,128)(2,1)}, u32[]{:S(2)}, u32[]{:S(2)}) collective-permute-start(bf16[384,640]{1,0:T(8,128)(2,1)} %get-tuple-element.256), channel_id=1, source_target_pairs={{0,2},{2,64},{64,66},{66,0},{1,3},{3,65},{65,67},{67,1},{4,6},{6,6... | collective-permute-start | bytes 1474568 | tf_op jit(solution)/shard_map/ppermute | solution.py:38
  89.4 30.6 %collective-permute-start.17 = (bf16[384,640]{1,0:T(8,128)(2,1)}, bf16[384,640]{1,0:T(8,128)(2,1)}, u32[]{:S(2)}, u32[]{:S(2)}) collective-permute-start(bf16[384,640]{1,0:T(8,128)(2,1)} %get-tuple-element.256), channel_id=1, source_target_pairs={{0,66},{2,0},{64,2},{66,64},{1,67},{3,1},{65,3},{67,65},{4,70},{6,... | collective-permute-start | bytes 1474568 | tf_op jit(solution)/shard_map/ppermute | solution.py:38
  92.7 17.7 %collective-permute-start.34 = (bf16[192,384]{1,0:T(8,128)(2,1)}, bf16[192,384]{1,0:T(8,128)(2,1)}, u32[]{:S(2)}, u32[]{:S(2)}) collective-permute-start(bf16[192,384]{1,0:T(8,128)(2,1)} %slice.1466), channel_id=1, source_target_pairs={{0,2},{2,64},{64,66},{66,0},{1,3},{3,65},{65,67},{67,1},{4,6},{6,6... | collective-permute-start | bytes 442376 | tf_op jit(solution)/shard_map/ppermute | solution.py:38
  110.3 43.2 %collective-permute-start.45 = (bf16[96,1792]{1,0:T(8,128)(2,1)}, bf16[96,1792]{1,0:T(8,128)(2,1)S(1)}, u32[]{:S(2)}, u32[]{:S(2)}) collective-permute-start(bf16[96,1792]{1,0:T(8,128)(2,1)} %get-tuple-element.141), channel_id=1, source_target_pairs={{0,4},{4,8},{8,12},{12,0},{1,5},{5,9},{9,13},{13,1},{2,6},{6,10},{... | collective-permute-start | bytes 1032200 | tf_op jit(solution)/shard_map/ppermute | solution.py:38
  110.5 45.8 %collective-permute-start.46 = (bf16[96,1792]{1,0:T(8,128)(2,1)}, bf16[96,1792]{1,0:T(8,128)(2,1)S(1)}, u32[]{:S(2)}, u32[]{:S(2)}) collective-permute-start(bf16[96,1792]{1,0:T(8,128)(2,1)} %get-tuple-element.141), channel_id=1, source_target_pairs={{0,12},{4,0},{8,4},{12,8},{1,13},{5,1},{9,5},{13,9},{2,14},{6,2},{... | collective-permute-start | bytes 1032200 | tf_op jit(solution)/shard_map/ppermute | solution.py:38
  128.9 37.7 %collective-permute-start.18 = (bf16[192,640]{1,0:T(8,128)(2,1)S(1)}, bf16[192,640]{1,0:T(8,128)(2,1)S(1)}, u32[]{:S(2)}, u32[]{:S(2)}) collective-permute-start(bf16[192,640]{1,0:T(8,128)(2,1)S(1)} %slice.1507), channel_id=1, source_target_pairs={{0,2},{2,64},{64,66},{66,0},{1,3},{3,65},{65,67},{67,1},{4,6},{6,6... | collective-permute-start | bytes 737288 | tf_op jit(solution)/shard_map/ppermute | solution.py:38
  130.4 39.6 %collective-permute-start.19 = (bf16[192,640]{1,0:T(8,128)(2,1)S(1)}, bf16[192,640]{1,0:T(8,128)(2,1)}, u32[]{:S(2)}, u32[]{:S(2)}) collective-permute-start(bf16[192,640]{1,0:T(8,128)(2,1)S(1)} %slice.1508), channel_id=1, source_target_pairs={{0,66},{2,0},{64,2},{66,64},{1,67},{3,1},{65,3},{67,65},{4,70},{6,... | collective-permute-start | bytes 737288 | tf_op jit(solution)/shard_map/ppermute | solution.py:38
  134.9 23.3 %collective-permute-start.55 = (bf16[48,1664]{1,0:T(8,128)(2,1)}, bf16[48,1664]{1,0:T(8,128)(2,1)S(1)}, u32[]{:S(2)}, u32[]{:S(2)}) collective-permute-start(bf16[48,1664]{1,0:T(8,128)(2,1)} %slice.1539), channel_id=1, source_target_pairs={{0,2},{2,64},{64,66},{66,0},{1,3},{3,65},{65,67},{67,1},{4,6},{6,6... | collective-permute-start | bytes 479240 | tf_op jit(solution)/shard_map/ppermute | solution.py:38
  162.4 36.0 %collective-permute-start.57 = (bf16[384,1664]{1,0:T(8,128)(2,1)}, bf16[384,1664]{1,0:T(8,128)(2,1)}, u32[]{:S(2)}, u32[]{:S(2)}) collective-permute-start(bf16[384,1664]{1,0:T(8,128)(2,1)} %constant_dynamic-update-slice_fusion.102), channel_id=1, source_target_pairs={{0,4},{4,8},{8,12},{12,0},{1,5},{5,9},{9,13},{13,1},{2,6},{6,10},{... | collective-permute-start | bytes 3833864 | tf_op jit(solution)/shard_map/ppermute | solution.py:38
  162.4 39.2 %collective-permute-start.58 = (bf16[384,1664]{1,0:T(8,128)(2,1)}, bf16[384,1664]{1,0:T(8,128)(2,1)}, u32[]{:S(2)}, u32[]{:S(2)}) collective-permute-start(bf16[384,1664]{1,0:T(8,128)(2,1)} %constant_dynamic-update-slice_fusion.102), channel_id=1, source_target_pairs={{0,12},{4,0},{8,4},{12,8},{1,13},{5,1},{9,5},{13,9},{2,14},{6,2},{... | collective-permute-start | bytes 3833864 | tf_op jit(solution)/shard_map/ppermute | solution.py:38
  166.6 39.1 %collective-permute-start.49 = (bf16[384,1792]{1,0:T(8,128)(2,1)}, bf16[384,1792]{1,0:T(8,128)(2,1)}, u32[]{:S(2)}, u32[]{:S(2)}) collective-permute-start(bf16[384,1792]{1,0:T(8,128)(2,1)} %get-tuple-element.224), channel_id=1, source_target_pairs={{0,2},{2,64},{64,66},{66,0},{1,3},{3,65},{65,67},{67,1},{4,6},{6,6... | collective-permute-start | bytes 4128776 | tf_op jit(solution)/shard_map/ppermute | solution.py:38
  166.6 43.5 %collective-permute-start.50 = (bf16[384,1792]{1,0:T(8,128)(2,1)}, bf16[384,1792]{1,0:T(8,128)(2,1)}, u32[]{:S(2)}, u32[]{:S(2)}) collective-permute-start(bf16[384,1792]{1,0:T(8,128)(2,1)} %get-tuple-element.224), channel_id=1, source_target_pairs={{0,66},{2,0},{64,2},{66,64},{1,67},{3,1},{65,3},{67,65},{4,70},{6,... | collective-permute-start | bytes 4128776 | tf_op jit(solution)/shard_map/ppermute | solution.py:38
  173.7 48.7 %collective-permute-start.20 = (bf16[1536,1024]{1,0:T(8,128)(2,1)S(1)}, bf16[1536,1024]{1,0:T(8,128)(2,1)}, u32[]{:S(2)}, u32[]{:S(2)}) collective-permute-start(bf16[1536,1024]{1,0:T(8,128)(2,1)S(1)} %pad_maximum_fusion.3), channel_id=1, source_target_pairs={{0,1},{1,0},{2,3},{3,2},{4,5},{5,4},{6,7},{7,6},{8,9},{9,8},{10,11... | collective-permute-start | bytes 9437192 | tf_op jit(solution)/shard_map/ppermute | solution.py:42
  198.4 64.5 %collective-permute-start.44 = (bf16[1536,768]{1,0:T(8,128)(2,1)}, bf16[1536,768]{1,0:T(8,128)(2,1)}, u32[]{:S(2)}, u32[]{:S(2)}) collective-permute-start(bf16[1536,768]{1,0:T(8,128)(2,1)} %pad_maximum_fusion.4), channel_id=1, source_target_pairs={{0,1},{1,0},{2,3},{3,2},{4,5},{5,4},{6,7},{7,6},{8,9},{9,8},{10,11... | collective-permute-start | bytes 7077896 | tf_op jit(solution)/shard_map/ppermute | solution.py:42
  205.7 69.9 %collective-permute-start.60 = (bf16[192,1664]{1,0:T(8,128)(2,1)}, bf16[192,1664]{1,0:T(8,128)(2,1)}, u32[]{:S(2)}, u32[]{:S(2)}) collective-permute-start(bf16[192,1664]{1,0:T(8,128)(2,1)} %slice.1550), channel_id=1, source_target_pairs={{0,12},{4,0},{8,4},{12,8},{1,13},{5,1},{9,5},{13,9},{2,14},{6,2},{... | collective-permute-start | bytes 1916936 | tf_op jit(solution)/shard_map/ppermute | solution.py:38
  210.1 73.7 %collective-permute-start.51 = (bf16[192,1792]{1,0:T(8,128)(2,1)}, bf16[192,1792]{1,0:T(8,128)(2,1)}, u32[]{:S(2)}, u32[]{:S(2)}) collective-permute-start(bf16[192,1792]{1,0:T(8,128)(2,1)} %slice.1535), channel_id=1, source_target_pairs={{0,2},{2,64},{64,66},{66,0},{1,3},{3,65},{65,67},{67,1},{4,6},{6,6... | collective-permute-start | bytes 2064392 | tf_op jit(solution)/shard_map/ppermute | solution.py:38
  251.0 34.9 %collective-permute-start.52 = (bf16[192,1792]{1,0:T(8,128)(2,1)S(1)}, bf16[192,1792]{1,0:T(8,128)(2,1)S(1)}, u32[]{:S(2)}, u32[]{:S(2)}) collective-permute-start(bf16[192,1792]{1,0:T(8,128)(2,1)S(1)} %copy-done.64), channel_id=1, source_target_pairs={{0,66},{2,0},{64,2},{66,64},{1,67},{3,1},{65,3},{67,65},{4,70},{6,... | collective-permute-start | bytes 2064392 | tf_op jit(solution)/shard_map/ppermute | solution.py:38
  268.4 221.0 %reduce-scatter.9.cloned.1.call-start = ((), (), s32[]{:S(2)}) async-start(), calls=%async_computation.7 | async-start | bytes 3538944
  333.5 61.2 %collective-permute-start.117 = (bf16[192,1792]{1,0:T(8,128)(2,1)}, bf16[192,1792]{1,0:T(8,128)(2,1)}, u32[]{:S(2)}, u32[]{:S(2)}) collective-permute-start(bf16[192,1792]{1,0:T(8,128)(2,1)} %copy.153), channel_id=1, source_target_pairs={{0,2},{2,64},{64,66},{66,0},{1,3},{3,65},{65,67},{67,1},{4,6},{6,6... | collective-permute-start | bytes 2064392 | tf_op jit(solution)/shard_map/ppermute | solution.py:38
  336.9 60.0 %collective-permute-start.119 = (bf16[192,1792]{1,0:T(8,128)(2,1)}, bf16[192,1792]{1,0:T(8,128)(2,1)}, u32[]{:S(2)}, u32[]{:S(2)}) collective-permute-start(bf16[192,1792]{1,0:T(8,128)(2,1)} %copy.155), channel_id=1, source_target_pairs={{0,66},{2,0},{64,2},{66,64},{1,67},{3,1},{65,3},{67,65},{4,70},{6,... | collective-permute-start | bytes 2064392 | tf_op jit(solution)/shard_map/ppermute | solution.py:38
  386.1 29.1 %collective-permute-start.126 = (bf16[384,1664]{0,1:T(8,128)(2,1)}, bf16[384,1664]{0,1:T(8,128)(2,1)}, u32[]{:S(2)}, u32[]{:S(2)}) collective-permute-start(bf16[384,1664]{0,1:T(8,128)(2,1)} %get-tuple-element.40), channel_id=1, source_target_pairs={{0,4},{4,8},{8,12},{12,0},{1,5},{5,9},{9,13},{13,1},{2,6},{6,10},{... | collective-permute-start | bytes 3833864 | tf_op jit(solution)/shard_map/ppermute | solution.py:38
  387.4 27.8 %collective-permute-start.128 = (bf16[384,1664]{0,1:T(8,128)(2,1)}, bf16[384,1664]{0,1:T(8,128)(2,1)}, u32[]{:S(2)}, u32[]{:S(2)}) collective-permute-start(bf16[384,1664]{0,1:T(8,128)(2,1)} %get-tuple-element.41), channel_id=1, source_target_pairs={{0,12},{4,0},{8,4},{12,8},{1,13},{5,1},{9,5},{13,9},{2,14},{6,2},{... | collective-permute-start | bytes 3833864 | tf_op jit(solution)/shard_map/ppermute | solution.py:38
  402.5 30.4 %collective-permute-start.118 = (bf16[384,1792]{0,1:T(8,128)(2,1)S(1)}, bf16[384,1792]{0,1:T(8,128)(2,1)S(1)}, u32[]{:S(2)}, u32[]{:S(2)}) collective-permute-start(bf16[384,1792]{0,1:T(8,128)(2,1)S(1)} %pad_maximum_fusion.5), channel_id=1, source_target_pairs={{0,2},{2,64},{64,66},{66,0},{1,3},{3,65},{65,67},{67,1},{4,6},{6,6... | collective-permute-start | bytes 4128776 | tf_op jit(solution)/shard_map/ppermute | solution.py:38
  403.6 29.2 %collective-permute-start.120 = (bf16[384,1792]{0,1:T(8,128)(2,1)S(1)}, bf16[384,1792]{0,1:T(8,128)(2,1)S(1)}, u32[]{:S(2)}, u32[]{:S(2)}) collective-permute-start(bf16[384,1792]{0,1:T(8,128)(2,1)S(1)} %pad_maximum_fusion.6), channel_id=1, source_target_pairs={{0,66},{2,0},{64,2},{66,64},{1,67},{3,1},{65,3},{67,65},{4,70},{6,... | collective-permute-start | bytes 4128776 | tf_op jit(solution)/shard_map/ppermute | solution.py:38
  457.3 22.7 %all-to-all-start.1 = ((bf16[8,16,3456]{2,1,0:T(8,128)(2,1)}), bf16[8,16,3456]{2,1,0:T(8,128)(2,1)S(1)}, u32[]{:S(2)}, u32[]{:S(2)}) async-start(bf16[8,16,3456]{2,1,0:T(8,128)(2,1)} %bitcast.86), calls=%async_computation.1 | async-start | bytes 1769472 | tf_op jit(solution)/shard_map/all_to_all | solution.py:370
  466.6 60.2 %reduce-scatter.7.cloned.1.call-start = ((), (), s32[]{:S(2)}) async-start(), calls=%async_computation.6 | async-start | bytes 3538944
  509.8 24.9 %collective-permute-start.61 = (bf16[128,512]{0,1:T(8,128)(2,1)}, bf16[128,512]{0,1:T(8,128)(2,1)S(1)}, u32[]{:S(2)}, u32[]{:S(2)}) collective-permute-start(bf16[128,512]{0,1:T(8,128)(2,1)} %get-tuple-element.102), channel_id=1, source_target_pairs={{0,16},{16,0},{32,48},{48,32},{64,80},{80,64},{96,112},{112,96},{1... | collective-permute-start | bytes 393224 | tf_op jit(solution)/shard_map/ppermute | solution.py:314
  510.3 28.9 %collective-permute-start.62 = (bf16[128,512]{0,1:T(8,128)(2,1)}, bf16[128,512]{0,1:T(8,128)(2,1)S(1)}, u32[]{:S(2)}, u32[]{:S(2)}) collective-permute-start(bf16[128,512]{0,1:T(8,128)(2,1)} %get-tuple-element.103), channel_id=1, source_target_pairs={{0,32},{16,48},{32,0},{48,16},{64,96},{80,112},{96,64},{112,80},{1... | collective-permute-start | bytes 393224 | tf_op jit(solution)/shard_map/ppermute | solution.py:314
  512.0 30.2 %collective-permute-start.63 = (bf16[128,512]{0,1:T(8,128)(2,1)}, bf16[128,512]{0,1:T(8,128)(2,1)}, u32[]{:S(2)}, u32[]{:S(2)}) collective-permute-start(bf16[128,512]{0,1:T(8,128)(2,1)} %get-tuple-element.104), channel_id=1, source_target_pairs={{0,48},{16,32},{32,16},{48,0},{64,112},{80,96},{96,80},{112,64},{1... | collective-permute-start | bytes 393224 | tf_op jit(solution)/shard_map/ppermute | solution.py:314
  513.7 30.7 %collective-permute-start.64 = (bf16[128,512]{0,1:T(8,128)(2,1)}, bf16[128,512]{0,1:T(8,128)(2,1)}, u32[]{:S(2)}, u32[]{:S(2)}) collective-permute-start(bf16[128,512]{0,1:T(8,128)(2,1)} %get-tuple-element.105), channel_id=1, source_target_pairs={{0,64},{16,80},{32,96},{48,112},{64,0},{80,16},{96,32},{112,48},{1... | collective-permute-start | bytes 393224 | tf_op jit(solution)/shard_map/ppermute | solution.py:314
  515.9 28.5 %collective-permute-start.65 = (bf16[128,512]{0,1:T(8,128)(2,1)}, bf16[128,512]{0,1:T(8,128)(2,1)}, u32[]{:S(2)}, u32[]{:S(2)}) collective-permute-start(bf16[128,512]{0,1:T(8,128)(2,1)} %get-tuple-element.106), channel_id=1, source_target_pairs={{0,80},{16,64},{32,112},{48,96},{64,16},{80,0},{96,48},{112,32},{1... | collective-permute-start | bytes 393224 | tf_op jit(solution)/shard_map/ppermute | solution.py:314
  542.2 52.7 %collective-permute-start.96 = (bf16[1536,768]{1,0:T(8,128)(2,1)}, bf16[1536,768]{1,0:T(8,128)(2,1)}, u32[]{:S(2)}, u32[]{:S(2)}) collective-permute-start(bf16[1536,768]{1,0:T(8,128)(2,1)} %convolution_convert_fusion.8), channel_id=1, source_target_pairs={{0,1},{1,0},{2,3},{3,2},{4,5},{5,4},{6,7},{7,6},{8,9},{9,8},{10,11... | collective-permute-start | bytes 7077896 | tf_op jit(solution)/shard_map/ppermute | solution.py:42
  572.1 64.3 %collective-permute-start.68 = (bf16[1536,1152]{0,1:T(8,128)(2,1)S(1)}, bf16[1536,1152]{0,1:T(8,128)(2,1)S(1)}, u32[]{:S(2)}, u32[]{:S(2)}) collective-permute-start(bf16[1536,1152]{0,1:T(8,128)(2,1)S(1)} %pad_maximum_fusion), channel_id=1, source_target_pairs={{0,1},{1,0},{2,3},{3,2},{4,5},{5,4},{6,7},{7,6},{8,9},{9,8},{10,11... | collective-permute-start | bytes 10616840 | tf_op jit(solution)/shard_map/ppermute | solution.py:42
  591.9 41.1 %collective-permute-start.95 = (f32[8,256]{1,0:T(8,128)S(1)}, f32[8,256]{1,0:T(8,128)S(1)}, u32[]{:S(2)}, u32[]{:S(2)}) collective-permute-start(f32[8,256]{1,0:T(8,128)S(1)} %add.951), channel_id=1, source_target_pairs={{0,8},{4,12},{8,0},{12,4},{1,9},{5,13},{9,1},{13,5},{2,10},{6,14},... | collective-permute-start | bytes 24584 | tf_op jit(solution)/shard_map/ppermute | solution.py:449
  651.6 23.5 %collective-permute-start.70 = (bf16[384,640]{0,1:T(8,128)(2,1)S(1)}, bf16[384,640]{0,1:T(8,128)(2,1)S(1)}, u32[]{:S(2)}, u32[]{:S(2)}) collective-permute-start(bf16[384,640]{0,1:T(8,128)(2,1)S(1)} %pad_maximum_fusion.11), channel_id=1, source_target_pairs={{0,2},{2,64},{64,66},{66,0},{1,3},{3,65},{65,67},{67,1},{4,6},{6,6... | collective-permute-start | bytes 1474568 | tf_op jit(solution)/shard_map/ppermute | solution.py:38
  651.9 23.3 %collective-permute-start.72 = (bf16[384,640]{0,1:T(8,128)(2,1)S(1)}, bf16[384,640]{0,1:T(8,128)(2,1)S(1)}, u32[]{:S(2)}, u32[]{:S(2)}) collective-permute-start(bf16[384,640]{0,1:T(8,128)(2,1)S(1)} %pad_maximum_fusion.12), channel_id=1, source_target_pairs={{0,66},{2,0},{64,2},{66,64},{1,67},{3,1},{65,3},{67,65},{4,70},{6,... | collective-permute-start | bytes 1474568 | tf_op jit(solution)/shard_map/ppermute | solution.py:38
  656.5 18.2 %collective-permute-start.81 = (bf16[48,512]{0,1:T(8,128)(2,1)S(1)}, bf16[48,512]{0,1:T(8,128)(2,1)S(1)}, u32[]{:S(2)}, u32[]{:S(2)}) collective-permute-start(bf16[48,512]{0,1:T(8,128)(2,1)S(1)} %get-tuple-element.159), channel_id=1, source_target_pairs={{0,2},{2,64},{64,66},{66,0},{1,3},{3,65},{65,67},{67,1},{4,6},{6,6... | collective-permute-start | bytes 147464 | tf_op jit(solution)/shard_map/ppermute | solution.py:38
  656.6 18.1 %collective-permute-start.83 = (bf16[48,512]{0,1:T(8,128)(2,1)S(1)}, bf16[48,512]{0,1:T(8,128)(2,1)S(1)}, u32[]{:S(2)}, u32[]{:S(2)}) collective-permute-start(bf16[48,512]{0,1:T(8,128)(2,1)S(1)} %get-tuple-element.160), channel_id=1, source_target_pairs={{0,66},{2,0},{64,2},{66,64},{1,67},{3,1},{65,3},{67,65},{4,70},{6,... | collective-permute-start | bytes 147464 | tf_op jit(solution)/shard_map/ppermute | solution.py:38
  659.2 33.0 %collective-permute-start.116 = (bf16[16,768]{1,0:T(8,128)(2,1)S(1)}, bf16[16,768]{1,0:T(8,128)(2,1)S(1)}, u32[]{:S(2)}, u32[]{:S(2)}) collective-permute-start(bf16[16,768]{1,0:T(8,128)(2,1)S(1)} %get-tuple-element.263), channel_id=1, source_target_pairs={{0,1},{1,0},{2,3},{3,2},{4,5},{5,4},{6,7},{7,6},{8,9},{9,8},{10,11... | collective-permute-start | bytes 73736 | tf_op jit(solution)/shard_map/ppermute | solution.py:42
  (238 other events, 2817.4 us)
Sparse Core Ops, SparseCore 0:
  34.0 34.2 all-gather.4
  268.5 32.7 all-gather.2
  394.9 33.5 reduce-scatter.8
  475.9 36.5 reduce-scatter.6
